TPU v7x, 32 devices: a whole 2x2x4 slice. The times are simulated.
32 devices in a mesh: gx: 2 (over y), gy: 4 (over x, core), gz: 4 (over z).
Axes of the slice: x: 2, y: 2, z: 4, core: 2. Of those that a mesh axis runs over, the one named last changes fastest.
Arguments:
- right_side: float32 [128, 64, 256], P('gz', 'gy', 'gx'), may hold values from -33 to 33
- initial: float32 [128, 64, 256], P('gz', 'gy', 'gx'), may hold values from -4 to 4
- kappa_sq: float32 [128, 64, 256], P('gz', 'gy', 'gx'), may hold values from 0.0004 to 4
Outputs:
- solution: float32 [128, 64, 256], P('gz', 'gy', 'gx')
- residual: float32 [128, 64, 256], P('gz', 'gy', 'gx')
All inputs are finite; a program needn't handle non-finite values.
Results may differ from a plain program's by a relative error of at most 0.0001.
Values sent between devices are 32-bit elements; how exact they have to be, the bound alone decides.
A program may use at most 64 MiB of HBM per device.

v0:
```python
import jax
import jax.numpy as jnp
from jax import lax
from jax.sharding import PartitionSpec as P

ITERS = 2
SWEEPS = 3


cheb_high = 7.2
cheb_low = 0.072


def padded_2(x, sides, width):
    for axis, dim in sides:
        devices, length = (lax.axis_size(axis), x.shape[dim])
        up = [(i, (i + 1) % devices) for i in range(devices - 1)]
        down = [(j, i) for i, j in up]
        last = lax.slice_in_dim(x, length - width, length, axis=dim)
        first = lax.slice_in_dim(x, 0, width, axis=dim)
        before = lax.ppermute(last, axis, up)
        after = lax.ppermute(first, axis, down)
        x = jnp.concatenate([before, x, after], axis=dim)
    return x


def neighbours(padded):
    total = padded[2:, 1:-1, 1:-1] + padded[:-2, 1:-1, 1:-1]
    total = total + padded[1:-1, 2:, 1:-1] + padded[1:-1, :-2, 1:-1]
    total = total + padded[1:-1, 1:-1, 2:] + padded[1:-1, 1:-1, :-2]
    return total


def axis_inside(count, axis_index, axis_size, margin):
    position = axis_index * count + jnp.arange(-margin, count + margin)
    return ((position >= 0) & (position < count * axis_size)).astype(jnp.float32)


def inside_mask(kappa_sq, margin):
    depth_cells, rows_cells, cols_cells = kappa_sq.shape
    inside_z = axis_inside(depth_cells, lax.axis_index("gz"), lax.axis_size("gz"), margin)
    inside_y = axis_inside(rows_cells, lax.axis_index("gy"), lax.axis_size("gy"), margin)
    inside_x = axis_inside(cols_cells, lax.axis_index("gx"), lax.axis_size("gx"), margin)
    return inside_z[:, None, None] * inside_y[None, :, None] * inside_x[None, None, :]


def crop_box(array_in, margin):
    return array_in[margin:-margin, margin:-margin, margin:-margin]


def precondition_box(source, q_box):
    centre = (cheb_high + cheb_low) / 2.0
    half_width = (cheb_high - cheb_low) / 2.0
    ratio_sigma = centre / half_width
    weight_old = 1.0 / ratio_sigma
    update = source / centre
    result = update
    for sweep in range(SWEEPS - 1):
        applied_box = q_box(result)
        source = crop_box(source, 2)
        update = crop_box(update, 2)
        result = crop_box(result, 2)
        defect = source - applied_box
        weight_new = 1.0 / (2.0 * ratio_sigma - weight_old)
        update = weight_new * weight_old * update + 2.0 * weight_new / half_width * defect
        result = result + update
        weight_old = weight_new
    return result


def global_dot(first_field, second_field):
    return lax.psum(jnp.sum(first_field * second_field), ("gx", "gy", "gz"))


def body(right_side, initial, kappa_sq):
    depth_all = 2 * SWEEPS
    mask_own = inside_mask(kappa_sq, 0)
    kappa_deep, mask_deep = (
        padded_2(kappa_sq, (("gx", 2), ("gy", 1), ("gz", 0)), depth_all),
        padded_2(mask_own, (("gx", 2), ("gy", 1), ("gz", 0)), depth_all),
    )

    def k_box(padded):
        margin = (kappa_deep.shape[0] - padded.shape[0]) // 2 + 1
        coef_box = crop_box(kappa_deep, margin)
        return (
            ((6.0 + coef_box) * crop_box(padded, 1) - neighbours(padded))
            / 6.0
            * crop_box(mask_deep, margin)
        )

    def q_box(padded):
        return k_box(k_box(padded))

    def deep_field(values, width):
        return padded_2(values, (("gx", 2), ("gy", 1), ("gz", 0)), width)

    def apply_q(values):
        return q_box(deep_field(values, 2))

    def precond_of(values):
        return precondition_box(deep_field(values, 2 * (SWEEPS - 1)), q_box)

    solution = initial
    residual = right_side - apply_q(initial)
    precond = precond_of(residual)
    direction = precond
    energy = global_dot(residual, precond)
    for step in range(ITERS):
        applied = apply_q(direction)
        step_size = energy / global_dot(direction, applied)
        solution = solution + step_size * direction
        residual = residual - step_size * applied
        if step + 1 < ITERS:
            precond = precond_of(residual)
            energy_new = global_dot(residual, precond)
            direction = precond + energy_new / energy * direction
            energy = energy_new
    return (solution, residual)


def solution(mesh):
    in_specs = (P("gz", "gy", "gx"), P("gz", "gy", "gx"), P("gz", "gy", "gx"))
    out_specs = (P("gz", "gy", "gx"), P("gz", "gy", "gx"))
    return jax.shard_map(body, mesh=mesh, in_specs=in_specs, out_specs=out_specs, check_vma=False)
```

profile of v0, /device:TPU:0, one launch (start us, length us, event | category | flops | bytes accessed | tf_op | source)
XLA Modules:
  0.0 332.2 jit_solution(7153482162157581981)
XLA Ops:
  1.1 4.9 %collective-permute-start.12 = (f32[32,16,6]{2,1,0:T(8,128)S(1)}, f32[32,16,6]{2,1,0:T(8,128)S(1)}, u32[]{:S(2)}, u32[]{:S(2)}) collective-permute-start(f32[32,16,6]{2,1,0:T(8,128)S(1)} %get-tuple-element.57), channel_id=1, source_target_pairs={{0,16},{1,17},{2,18},{3,19},{4,20},{5,21},{6,22},{7,23},{8,24},{9,... | collective-permute-start | bytes 36872 | tf_op jit(solution)/shard_map/ppermute | solution.py:21
  5.9 1.3 collective-permute-start.13
  7.4 4.6 %collective-permute-start.6 = (f32[32,16,2]{2,1,0:T(8,128)S(1)}, f32[32,16,2]{2,1,0:T(8,128)S(1)}, u32[]{:S(2)}, u32[]{:S(2)}) collective-permute-start(f32[32,16,2]{2,1,0:T(8,128)S(1)} %get-tuple-element.59), channel_id=1, source_target_pairs={{0,16},{1,17},{2,18},{3,19},{4,20},{5,21},{6,22},{7,23},{8,24},{9,... | collective-permute-start | bytes 12296 | tf_op jit(solution)/shard_map/ppermute | solution.py:21
  12.0 1.3 collective-permute-start.7
  13.4 4.6 %collective-permute-start = (f32[32,16,6]{2,1,0:T(8,128)S(1)}, f32[32,16,6]{2,1,0:T(8,128)S(1)}, u32[]{:S(2)}, u32[]{:S(2)}) collective-permute-start(f32[32,16,6]{2,1,0:T(8,128)S(1)} %get-tuple-element.55), channel_id=1, source_target_pairs={{0,16},{1,17},{2,18},{3,19},{4,20},{5,21},{6,22},{7,23},{8,24},{9,... | collective-permute-start | bytes 36872 | tf_op jit(solution)/shard_map/ppermute | solution.py:21
  18.0 1.3 collective-permute-start.1
  19.3 2.1 collective-permute-done.7
  21.7 1.3 collective-permute-start.8
  23.0 1.3 collective-permute-start.9
  24.7 4.8 %collective-permute-start.14 = (f32[32,6,140]{2,1,0:T(8,128)S(1)}, f32[32,6,140]{2,1,0:T(8,128)S(1)}, u32[]{:S(2)}, u32[]{:S(2)}) collective-permute-start(f32[32,6,140]{2,1,0:T(8,128)S(1)} %get-tuple-element.45), channel_id=1, source_target_pairs={{0,4},{4,8},{8,12},{1,5},{5,9},{9,13},{2,6},{6,10},{10,14},{3,7},{... | collective-permute-start | bytes 322568 | tf_op jit(solution)/shard_map/ppermute | solution.py:21
  29.5 1.3 collective-permute-start.15
  31.2 3.5 %collective-permute-start.10 = (f32[2,20,132]{2,1,0:T(8,128)S(1)}, f32[2,20,132]{2,1,0:T(8,128)S(1)}, u32[]{:S(2)}, u32[]{:S(2)}) collective-permute-start(f32[2,20,132]{2,1,0:T(8,128)S(1)} %get-tuple-element.31), channel_id=1, source_target_pairs={{0,1},{1,2},{2,3},{4,5},{5,6},{6,7},{8,9},{9,10},{10,11},{12,13},{... | collective-permute-start | bytes 63368 | tf_op jit(solution)/shard_map/ppermute | solution.py:21
  36.0 4.0 %collective-permute-start.2 = (f32[32,6,140]{2,1,0:T(8,128)S(1)}, f32[32,6,140]{2,1,0:T(8,128)S(1)}, u32[]{:S(2)}, u32[]{:S(2)}) collective-permute-start(f32[32,6,140]{2,1,0:T(8,128)S(1)} %get-tuple-element.43), channel_id=1, source_target_pairs={{0,4},{4,8},{8,12},{1,5},{5,9},{9,13},{2,6},{6,10},{10,14},{3,7},{... | collective-permute-start | bytes 322568 | tf_op jit(solution)/shard_map/ppermute | solution.py:21
  41.9 4.3 %collective-permute-start.16 = (f32[6,28,140]{2,1,0:T(8,128)S(1)}, f32[6,28,140]{2,1,0:T(8,128)S(1)}, u32[]{:S(2)}, u32[]{:S(2)}) collective-permute-start(f32[6,28,140]{2,1,0:T(8,128)S(1)} %get-tuple-element.21), channel_id=1, source_target_pairs={{0,1},{1,2},{2,3},{4,5},{5,6},{6,7},{8,9},{9,10},{10,11},{12,13},{... | collective-permute-start | bytes 282248 | tf_op jit(solution)/shard_map/ppermute | solution.py:21
  47.7 4.6 %collective-permute-start.4 = (f32[6,28,140]{2,1,0:T(8,128)S(1)}, f32[6,28,140]{2,1,0:T(8,128)S(1)}, u32[]{:S(2)}, u32[]{:S(2)}) collective-permute-start(f32[6,28,140]{2,1,0:T(8,128)S(1)} %get-tuple-element.19), channel_id=1, source_target_pairs={{0,1},{1,2},{2,3},{4,5},{5,6},{6,7},{8,9},{9,10},{10,11},{12,13},{... | collective-permute-start | bytes 282248 | tf_op jit(solution)/shard_map/ppermute | solution.py:21
  52.3 1.3 collective-permute-start.5
  54.6 1.6 collective-permute-done.4
  56.1 4.7 %collective-permute-done.5 = f32[6,28,140]{2,1,0:T(8,128)S(1)} collective-permute-done((f32[6,28,140]{2,1,0:T(8,128)S(1)}, f32[6,28,140]{2,1,0:T(8,128)S(1)}, u32[]{:S(2)}, u32[]{:S(2)}) %collective-permute-start.5) | collective-permute-done | bytes 94112 | tf_op jit(solution)/shard_map/ppermute | solution.py:22
  61.3 2.5 fusion.34
  64.5 2.4 collective-permute-start.18
  68.3 5.4 %collective-permute-done.18 = f32[32,16,4]{2,1,0:T(8,128)S(1)} collective-permute-done((f32[32,16,4]{2,1,0:T(8,128)S(1)}, f32[32,16,4]{2,1,0:T(8,128)S(1)}, u32[]{:S(2)}, u32[]{:S(2)}) %collective-permute-start.18) | collective-permute-done | bytes 8224 | tf_op jit(solution)/shard_map/ppermute | solution.py:21
  73.6 4.1 %collective-permute-done.19 = f32[32,16,4]{2,1,0:T(8,128)S(1)} collective-permute-done((f32[32,16,4]{2,1,0:T(8,128)S(1)}, f32[32,16,4]{2,1,0:T(8,128)S(1)}, u32[]{:S(2)}, u32[]{:S(2)}) %collective-permute-start.19) | collective-permute-done | bytes 8224 | tf_op jit(solution)/shard_map/ppermute | solution.py:22
  78.0 1.7 collective-permute-start.20
  81.0 2.8 collective-permute-done.21
  84.0 3.5 %collective-permute-start.22 = (f32[4,24,136]{2,1,0:T(8,128)S(1)}, f32[4,24,136]{2,1,0:T(8,128)S(1)}, u32[]{:S(2)}, u32[]{:S(2)}) collective-permute-start(f32[4,24,136]{2,1,0:T(8,128)S(1)} %get-tuple-element.25), channel_id=1, source_target_pairs={{0,1},{1,2},{2,3},{4,5},{5,6},{6,7},{8,9},{9,10},{10,11},{12,13},{... | collective-permute-start | bytes 156680 | tf_op jit(solution)/shard_map/ppermute | solution.py:21
  87.4 1.5 collective-permute-start.23
  89.6 4.3 %collective-permute-done.23 = f32[4,24,136]{2,1,0:T(8,128)S(1)} collective-permute-done((f32[4,24,136]{2,1,0:T(8,128)S(1)}, f32[4,24,136]{2,1,0:T(8,128)S(1)}, u32[]{:S(2)}, u32[]{:S(2)}) %collective-permute-start.23) | collective-permute-done | bytes 52256 | tf_op jit(solution)/shard_map/ppermute | solution.py:22
  94.4 2.0 fusion.5
  96.4 2.4 slice_add_fusion.46
  98.8 1.8 fusion.31
  101.5 1.5 collective-permute-start.24
  104.3 4.1 %collective-permute-done.24 = f32[32,16,2]{2,1,0:T(8,128)S(1)} collective-permute-done((f32[32,16,2]{2,1,0:T(8,128)S(1)}, f32[32,16,2]{2,1,0:T(8,128)S(1)}, u32[]{:S(2)}, u32[]{:S(2)}) %collective-permute-start.24) | collective-permute-done | bytes 4128 | tf_op jit(solution)/shard_map/ppermute | solution.py:21
  108.3 4.7 %collective-permute-done.25 = f32[32,16,2]{2,1,0:T(8,128)S(1)} collective-permute-done((f32[32,16,2]{2,1,0:T(8,128)S(1)}, f32[32,16,2]{2,1,0:T(8,128)S(1)}, u32[]{:S(2)}, u32[]{:S(2)}) %collective-permute-start.25) | collective-permute-done | bytes 4128 | tf_op jit(solution)/shard_map/ppermute | solution.py:22
  113.3 2.7 collective-permute-start.26
  117.4 2.1 collective-permute-done.27
  119.6 3.5 %collective-permute-start.28 = (f32[2,20,132]{2,1,0:T(8,128)S(1)}, f32[2,20,132]{2,1,0:T(8,128)S(1)}, u32[]{:S(2)}, u32[]{:S(2)}) collective-permute-start(f32[2,20,132]{2,1,0:T(8,128)S(1)} %get-tuple-element.29), channel_id=1, source_target_pairs={{0,1},{1,2},{2,3},{4,5},{5,6},{6,7},{8,9},{9,10},{10,11},{12,13},{... | collective-permute-start | bytes 63368 | tf_op jit(solution)/shard_map/ppermute | solution.py:21
  123.1 1.3 collective-permute-start.29
  124.8 4.3 %collective-permute-done.29 = f32[2,20,132]{2,1,0:T(8,128)S(1)} collective-permute-done((f32[2,20,132]{2,1,0:T(8,128)S(1)}, f32[2,20,132]{2,1,0:T(8,128)S(1)}, u32[]{:S(2)}, u32[]{:S(2)}) %collective-permute-start.29) | collective-permute-done | bytes 21152 | tf_op jit(solution)/shard_map/ppermute | solution.py:22
  129.5 2.5 fusion.27
  132.0 1.9 multiply_reduce_fusion.2
  133.9 39.0 %all-reduce = (f32[]{:T(128)}, f32[]{:T(128)}) all-reduce(f32[]{:T(128)} %get-tuple-element.3, f32[]{:T(128)} %get-tuple-element.2), channel_id=1, replica_groups=mesh['gx'=2,'gy'=4,'gz'=4] {'gx','gy','gz'}, use_global_device_ids=true, to_apply=%region_1.0 | all-reduce | flops 2 | bytes 16 | tf_op jit(solution)/shard_map/psum | solution.py:72
  175.5 4.5 %collective-permute-start.30 = (f32[32,16,4]{2,1,0:T(8,128)S(1)}, f32[32,16,4]{2,1,0:T(8,128)S(1)}, u32[]{:S(2)}, u32[]{:S(2)}) collective-permute-start(f32[32,16,4]{2,1,0:T(8,128)S(1)} %get-tuple-element.49), channel_id=1, source_target_pairs={{0,16},{1,17},{2,18},{3,19},{4,20},{5,21},{6,22},{7,23},{8,24},{9,... | collective-permute-start | bytes 24584 | tf_op jit(solution)/shard_map/ppermute | solution.py:21
  181.3 3.9 %collective-permute-done.30 = f32[32,16,4]{2,1,0:T(8,128)S(1)} collective-permute-done((f32[32,16,4]{2,1,0:T(8,128)S(1)}, f32[32,16,4]{2,1,0:T(8,128)S(1)}, u32[]{:S(2)}, u32[]{:S(2)}) %collective-permute-start.30) | collective-permute-done | bytes 8224 | tf_op jit(solution)/shard_map/ppermute | solution.py:21
  185.1 4.1 %collective-permute-done.31 = f32[32,16,4]{2,1,0:T(8,128)S(1)} collective-permute-done((f32[32,16,4]{2,1,0:T(8,128)S(1)}, f32[32,16,4]{2,1,0:T(8,128)S(1)}, u32[]{:S(2)}, u32[]{:S(2)}) %collective-permute-start.31) | collective-permute-done | bytes 8224 | tf_op jit(solution)/shard_map/ppermute | solution.py:22
  189.5 1.3 collective-permute-start.32
  192.2 3.0 collective-permute-done.33
  195.3 3.9 %collective-permute-start.34 = (f32[4,24,136]{2,1,0:T(8,128)S(1)}, f32[4,24,136]{2,1,0:T(8,128)S(1)}, u32[]{:S(2)}, u32[]{:S(2)}) collective-permute-start(f32[4,24,136]{2,1,0:T(8,128)S(1)} %get-tuple-element.23), channel_id=1, source_target_pairs={{0,1},{1,2},{2,3},{4,5},{5,6},{6,7},{8,9},{9,10},{10,11},{12,13},{... | collective-permute-start | bytes 156680 | tf_op jit(solution)/shard_map/ppermute | solution.py:21
  201.5 4.3 %collective-permute-done.35 = f32[4,24,136]{2,1,0:T(8,128)S(1)} collective-permute-done((f32[4,24,136]{2,1,0:T(8,128)S(1)}, f32[4,24,136]{2,1,0:T(8,128)S(1)}, u32[]{:S(2)}, u32[]{:S(2)}) %collective-permute-start.35) | collective-permute-done | bytes 52256 | tf_op jit(solution)/shard_map/ppermute | solution.py:22
  206.2 2.0 fusion.2
  208.2 2.4 slice_add_fusion.45
  210.7 1.8 fusion.24
  212.5 2.0 multiply_reduce_fusion.1
  214.5 39.8 %psum.30 = f32[]{:T(128)} all-reduce(f32[]{:T(128)} %get-tuple-element.8), channel_id=1, replica_groups=mesh['gx'=2,'gy'=4,'gz'=4] {'gx','gy','gz'}, use_global_device_ids=true, to_apply=%region_5.0 | all-reduce | flops 1 | bytes 8 | tf_op jit(solution)/shard_map/psum | solution.py:72
  256.7 4.4 %collective-permute-start.36 = (f32[32,16,2]{2,1,0:T(8,128)S(1)}, f32[32,16,2]{2,1,0:T(8,128)S(1)}, u32[]{:S(2)}, u32[]{:S(2)}) collective-permute-start(f32[32,16,2]{2,1,0:T(8,128)S(1)} %get-tuple-element.47), channel_id=1, source_target_pairs={{0,16},{1,17},{2,18},{3,19},{4,20},{5,21},{6,22},{7,23},{8,24},{9,... | collective-permute-start | bytes 12296 | tf_op jit(solution)/shard_map/ppermute | solution.py:21
  262.4 3.9 %collective-permute-done.36 = f32[32,16,2]{2,1,0:T(8,128)S(1)} collective-permute-done((f32[32,16,2]{2,1,0:T(8,128)S(1)}, f32[32,16,2]{2,1,0:T(8,128)S(1)}, u32[]{:S(2)}, u32[]{:S(2)}) %collective-permute-start.36) | collective-permute-done | bytes 4128 | tf_op jit(solution)/shard_map/ppermute | solution.py:21
  266.3 4.1 %collective-permute-done.37 = f32[32,16,2]{2,1,0:T(8,128)S(1)} collective-permute-done((f32[32,16,2]{2,1,0:T(8,128)S(1)}, f32[32,16,2]{2,1,0:T(8,128)S(1)}, u32[]{:S(2)}, u32[]{:S(2)}) %collective-permute-start.37) | collective-permute-done | bytes 4128 | tf_op jit(solution)/shard_map/ppermute | solution.py:22
  270.7 1.3 collective-permute-start.38
  273.4 3.0 collective-permute-done.39
  276.4 3.3 collective-permute-start.40
  279.7 1.6 collective-permute-start.41
  281.4 4.3 %collective-permute-done.41 = f32[2,20,132]{2,1,0:T(8,128)S(1)} collective-permute-done((f32[2,20,132]{2,1,0:T(8,128)S(1)}, f32[2,20,132]{2,1,0:T(8,128)S(1)}, u32[]{:S(2)}, u32[]{:S(2)}) %collective-permute-start.41) | collective-permute-done | bytes 21152 | tf_op jit(solution)/shard_map/ppermute | solution.py:22
  286.1 2.5 fusion.20
  289.8 39.3 %psum.31 = f32[]{:T(128)} all-reduce(f32[]{:T(128)} %get-tuple-element.6), channel_id=1, replica_groups=mesh['gx'=2,'gy'=4,'gz'=4] {'gx','gy','gz'}, use_global_device_ids=true, to_apply=%region_7.0 | all-reduce | flops 1 | bytes 8 | tf_op jit(solution)/shard_map/psum | solution.py:72
  330.4 1.8 multiply_subtract_fusion
  (91 shorter events, 29.6 us)
Async XLA Ops:
  0.6 6.6 %copy-start.5 = (f32[32,16,128]{2,1,0:T(8,128)S(1)}, f32[32,16,128]{2,1,0:T(8,128)}, u32[]{:S(2)}) copy-start(f32[32,16,128]{2,1,0:T(8,128)} %param.4) | copy-start | bytes 786436
  0.6 12.6 %copy-start = (f32[32,16,128]{2,1,0:T(8,128)S(1)}, f32[32,16,128]{2,1,0:T(8,128)}, u32[]{:S(2)}) copy-start(f32[32,16,128]{2,1,0:T(8,128)} %param.5) | copy-start | bytes 786436
  1.1 22.0 %collective-permute-start.12 = (f32[32,16,6]{2,1,0:T(8,128)S(1)}, f32[32,16,6]{2,1,0:T(8,128)S(1)}, u32[]{:S(2)}, u32[]{:S(2)}) collective-permute-start(f32[32,16,6]{2,1,0:T(8,128)S(1)} %get-tuple-element.57), channel_id=1, source_target_pairs={{0,16},{1,17},{2,18},{3,19},{4,20},{5,21},{6,22},{7,23},{8,24},{9,... | collective-permute-start | bytes 36872 | tf_op jit(solution)/shard_map/ppermute | solution.py:21
  5.9 18.4 %collective-permute-start.13 = (f32[32,16,6]{2,1,0:T(8,128)S(1)}, f32[32,16,6]{2,1,0:T(8,128)S(1)}, u32[]{:S(2)}, u32[]{:S(2)}) collective-permute-start(f32[32,16,6]{2,1,0:T(8,128)S(1)} %get-tuple-element.58), channel_id=1, source_target_pairs={{16,0},{17,1},{18,2},{19,3},{20,4},{21,5},{22,6},{23,7},{24,8},{25... | collective-permute-start | bytes 36872 | tf_op jit(solution)/shard_map/ppermute | solution.py:22
  7.4 10.6 %collective-permute-start.6 = (f32[32,16,2]{2,1,0:T(8,128)S(1)}, f32[32,16,2]{2,1,0:T(8,128)S(1)}, u32[]{:S(2)}, u32[]{:S(2)}) collective-permute-start(f32[32,16,2]{2,1,0:T(8,128)S(1)} %get-tuple-element.59), channel_id=1, source_target_pairs={{0,16},{1,17},{2,18},{3,19},{4,20},{5,21},{6,22},{7,23},{8,24},{9,... | collective-permute-start | bytes 12296 | tf_op jit(solution)/shard_map/ppermute | solution.py:21
  12.0 9.5 %collective-permute-start.7 = (f32[32,16,2]{2,1,0:T(8,128)S(1)}, f32[32,16,2]{2,1,0:T(8,128)S(1)}, u32[]{:S(2)}, u32[]{:S(2)}) collective-permute-start(f32[32,16,2]{2,1,0:T(8,128)S(1)} %get-tuple-element.60), channel_id=1, source_target_pairs={{16,0},{17,1},{18,2},{19,3},{20,4},{21,5},{22,6},{23,7},{24,8},{25... | collective-permute-start | bytes 12296 | tf_op jit(solution)/shard_map/ppermute | solution.py:22
  13.4 16.0 %collective-permute-start = (f32[32,16,6]{2,1,0:T(8,128)S(1)}, f32[32,16,6]{2,1,0:T(8,128)S(1)}, u32[]{:S(2)}, u32[]{:S(2)}) collective-permute-start(f32[32,16,6]{2,1,0:T(8,128)S(1)} %get-tuple-element.55), channel_id=1, source_target_pairs={{0,16},{1,17},{2,18},{3,19},{4,20},{5,21},{6,22},{7,23},{8,24},{9,... | collective-permute-start | bytes 36872 | tf_op jit(solution)/shard_map/ppermute | solution.py:21
  18.0 12.7 %collective-permute-start.1 = (f32[32,16,6]{2,1,0:T(8,128)S(1)}, f32[32,16,6]{2,1,0:T(8,128)S(1)}, u32[]{:S(2)}, u32[]{:S(2)}) collective-permute-start(f32[32,16,6]{2,1,0:T(8,128)S(1)} %get-tuple-element.56), channel_id=1, source_target_pairs={{16,0},{17,1},{18,2},{19,3},{20,4},{21,5},{22,6},{23,7},{24,8},{25... | collective-permute-start | bytes 36872 | tf_op jit(solution)/shard_map/ppermute | solution.py:22
  21.7 9.3 %collective-permute-start.8 = (f32[32,2,132]{2,1,0:T(2,128)S(1)}, f32[32,2,132]{2,1,0:T(2,128)S(1)}, u32[]{:S(2)}, u32[]{:S(2)}) collective-permute-start(f32[32,2,132]{2,1,0:T(2,128)S(1)} %get-tuple-element.41), channel_id=1, source_target_pairs={{0,4},{4,8},{8,12},{1,5},{5,9},{9,13},{2,6},{6,10},{10,14},{3,7},{... | collective-permute-start | bytes 101384 | tf_op jit(solution)/shard_map/ppermute | solution.py:21
  23.0 8.0 %collective-permute-start.9 = (f32[32,2,132]{2,1,0:T(2,128)S(1)}, f32[32,2,132]{2,1,0:T(2,128)S(1)}, u32[]{:S(2)}, u32[]{:S(2)}) collective-permute-start(f32[32,2,132]{2,1,0:T(2,128)S(1)} %get-tuple-element.42), channel_id=1, source_target_pairs={{4,0},{8,4},{12,8},{5,1},{9,5},{13,9},{6,2},{10,6},{14,10},{7,3},{... | collective-permute-start | bytes 101384 | tf_op jit(solution)/shard_map/ppermute | solution.py:22
  24.7 17.1 %collective-permute-start.14 = (f32[32,6,140]{2,1,0:T(8,128)S(1)}, f32[32,6,140]{2,1,0:T(8,128)S(1)}, u32[]{:S(2)}, u32[]{:S(2)}) collective-permute-start(f32[32,6,140]{2,1,0:T(8,128)S(1)} %get-tuple-element.45), channel_id=1, source_target_pairs={{0,4},{4,8},{8,12},{1,5},{5,9},{9,13},{2,6},{6,10},{10,14},{3,7},{... | collective-permute-start | bytes 322568 | tf_op jit(solution)/shard_map/ppermute | solution.py:21
  29.5 12.3 %collective-permute-start.15 = (f32[32,6,140]{2,1,0:T(8,128)S(1)}, f32[32,6,140]{2,1,0:T(8,128)S(1)}, u32[]{:S(2)}, u32[]{:S(2)}) collective-permute-start(f32[32,6,140]{2,1,0:T(8,128)S(1)} %get-tuple-element.46), channel_id=1, source_target_pairs={{4,0},{8,4},{12,8},{5,1},{9,5},{13,9},{6,2},{10,6},{14,10},{7,3},{... | collective-permute-start | bytes 322568 | tf_op jit(solution)/shard_map/ppermute | solution.py:22
  31.2 8.8 %collective-permute-start.10 = (f32[2,20,132]{2,1,0:T(8,128)S(1)}, f32[2,20,132]{2,1,0:T(8,128)S(1)}, u32[]{:S(2)}, u32[]{:S(2)}) collective-permute-start(f32[2,20,132]{2,1,0:T(8,128)S(1)} %get-tuple-element.31), channel_id=1, source_target_pairs={{0,1},{1,2},{2,3},{4,5},{5,6},{6,7},{8,9},{9,10},{10,11},{12,13},{... | collective-permute-start | bytes 63368 | tf_op jit(solution)/shard_map/ppermute | solution.py:21
  34.7 6.7 %collective-permute-start.11 = (f32[2,20,132]{2,1,0:T(8,128)S(1)}, f32[2,20,132]{2,1,0:T(8,128)S(1)}, u32[]{:S(2)}, u32[]{:S(2)}) collective-permute-start(f32[2,20,132]{2,1,0:T(8,128)S(1)} %get-tuple-element.32), channel_id=1, source_target_pairs={{1,0},{2,1},{3,2},{5,4},{6,5},{7,6},{9,8},{10,9},{11,10},{13,12},{... | collective-permute-start | bytes 63368 | tf_op jit(solution)/shard_map/ppermute | solution.py:22
  36.0 11.5 %collective-permute-start.2 = (f32[32,6,140]{2,1,0:T(8,128)S(1)}, f32[32,6,140]{2,1,0:T(8,128)S(1)}, u32[]{:S(2)}, u32[]{:S(2)}) collective-permute-start(f32[32,6,140]{2,1,0:T(8,128)S(1)} %get-tuple-element.43), channel_id=1, source_target_pairs={{0,4},{4,8},{8,12},{1,5},{5,9},{9,13},{2,6},{6,10},{10,14},{3,7},{... | collective-permute-start | bytes 322568 | tf_op jit(solution)/shard_map/ppermute | solution.py:21
  40.0 7.5 %collective-permute-start.3 = (f32[32,6,140]{2,1,0:T(8,128)S(1)}, f32[32,6,140]{2,1,0:T(8,128)S(1)}, u32[]{:S(2)}, u32[]{:S(2)}) collective-permute-start(f32[32,6,140]{2,1,0:T(8,128)S(1)} %get-tuple-element.44), channel_id=1, source_target_pairs={{4,0},{8,4},{12,8},{5,1},{9,5},{13,9},{6,2},{10,6},{14,10},{7,3},{... | collective-permute-start | bytes 322568 | tf_op jit(solution)/shard_map/ppermute | solution.py:22
  41.9 11.7 %collective-permute-start.16 = (f32[6,28,140]{2,1,0:T(8,128)S(1)}, f32[6,28,140]{2,1,0:T(8,128)S(1)}, u32[]{:S(2)}, u32[]{:S(2)}) collective-permute-start(f32[6,28,140]{2,1,0:T(8,128)S(1)} %get-tuple-element.21), channel_id=1, source_target_pairs={{0,1},{1,2},{2,3},{4,5},{5,6},{6,7},{8,9},{9,10},{10,11},{12,13},{... | collective-permute-start | bytes 282248 | tf_op jit(solution)/shard_map/ppermute | solution.py:21
  46.2 7.9 %collective-permute-start.17 = (f32[6,28,140]{2,1,0:T(8,128)S(1)}, f32[6,28,140]{2,1,0:T(8,128)S(1)}, u32[]{:S(2)}, u32[]{:S(2)}) collective-permute-start(f32[6,28,140]{2,1,0:T(8,128)S(1)} %get-tuple-element.22), channel_id=1, source_target_pairs={{1,0},{2,1},{3,2},{5,4},{6,5},{7,6},{9,8},{10,9},{11,10},{13,12},{... | collective-permute-start | bytes 282248 | tf_op jit(solution)/shard_map/ppermute | solution.py:22
  47.7 8.4 %collective-permute-start.4 = (f32[6,28,140]{2,1,0:T(8,128)S(1)}, f32[6,28,140]{2,1,0:T(8,128)S(1)}, u32[]{:S(2)}, u32[]{:S(2)}) collective-permute-start(f32[6,28,140]{2,1,0:T(8,128)S(1)} %get-tuple-element.19), channel_id=1, source_target_pairs={{0,1},{1,2},{2,3},{4,5},{5,6},{6,7},{8,9},{9,10},{10,11},{12,13},{... | collective-permute-start | bytes 282248 | tf_op jit(solution)/shard_map/ppermute | solution.py:21
  52.3 8.6 %collective-permute-start.5 = (f32[6,28,140]{2,1,0:T(8,128)S(1)}, f32[6,28,140]{2,1,0:T(8,128)S(1)}, u32[]{:S(2)}, u32[]{:S(2)}) collective-permute-start(f32[6,28,140]{2,1,0:T(8,128)S(1)} %get-tuple-element.20), channel_id=1, source_target_pairs={{1,0},{2,1},{3,2},{5,4},{6,5},{7,6},{9,8},{10,9},{11,10},{13,12},{... | collective-permute-start | bytes 282248 | tf_op jit(solution)/shard_map/ppermute | solution.py:22
  61.2 2.5 copy-start.7
  64.4 67.6 %copy-start.1 = (f32[32,16,128]{2,1,0:T(8,128)}, f32[32,16,128]{2,1,0:T(8,128)S(1)}, u32[]{:S(2)}) copy-start(f32[32,16,128]{2,1,0:T(8,128)S(1)} %fusion.36) | copy-start | bytes 786436
  64.5 9.1 %collective-permute-start.18 = (f32[32,16,4]{2,1,0:T(8,128)S(1)}, f32[32,16,4]{2,1,0:T(8,128)S(1)}, u32[]{:S(2)}, u32[]{:S(2)}) collective-permute-start(f32[32,16,4]{2,1,0:T(8,128)S(1)} %get-tuple-element.53), channel_id=1, source_target_pairs={{0,16},{1,17},{2,18},{3,19},{4,20},{5,21},{6,22},{7,23},{8,24},{9,... | collective-permute-start | bytes 24584 | tf_op jit(solution)/shard_map/ppermute | solution.py:21
  67.0 10.8 %collective-permute-start.19 = (f32[32,16,4]{2,1,0:T(8,128)S(1)}, f32[32,16,4]{2,1,0:T(8,128)S(1)}, u32[]{:S(2)}, u32[]{:S(2)}) collective-permute-start(f32[32,16,4]{2,1,0:T(8,128)S(1)} %get-tuple-element.54), channel_id=1, source_target_pairs={{16,0},{17,1},{18,2},{19,3},{20,4},{21,5},{22,6},{23,7},{24,8},{25... | collective-permute-start | bytes 24584 | tf_op jit(solution)/shard_map/ppermute | solution.py:22
  78.0 3.0 collective-permute-start.20
  79.7 4.1 %collective-permute-start.21 = (f32[32,4,136]{2,1,0:T(4,128)S(1)}, f32[32,4,136]{2,1,0:T(4,128)S(1)}, u32[]{:S(2)}, u32[]{:S(2)}) collective-permute-start(f32[32,4,136]{2,1,0:T(4,128)S(1)} %get-tuple-element.40), channel_id=1, source_target_pairs={{4,0},{8,4},{12,8},{5,1},{9,5},{13,9},{6,2},{10,6},{14,10},{7,3},{... | collective-permute-start | bytes 208904 | tf_op jit(solution)/shard_map/ppermute | solution.py:22
  84.0 5.7 %collective-permute-start.22 = (f32[4,24,136]{2,1,0:T(8,128)S(1)}, f32[4,24,136]{2,1,0:T(8,128)S(1)}, u32[]{:S(2)}, u32[]{:S(2)}) collective-permute-start(f32[4,24,136]{2,1,0:T(8,128)S(1)} %get-tuple-element.25), channel_id=1, source_target_pairs={{0,1},{1,2},{2,3},{4,5},{5,6},{6,7},{8,9},{9,10},{10,11},{12,13},{... | collective-permute-start | bytes 156680 | tf_op jit(solution)/shard_map/ppermute | solution.py:21
  87.4 6.5 %collective-permute-start.23 = (f32[4,24,136]{2,1,0:T(8,128)S(1)}, f32[4,24,136]{2,1,0:T(8,128)S(1)}, u32[]{:S(2)}, u32[]{:S(2)}) collective-permute-start(f32[4,24,136]{2,1,0:T(8,128)S(1)} %get-tuple-element.26), channel_id=1, source_target_pairs={{1,0},{2,1},{3,2},{5,4},{6,5},{7,6},{9,8},{10,9},{11,10},{13,12},{... | collective-permute-start | bytes 156680 | tf_op jit(solution)/shard_map/ppermute | solution.py:22
  101.5 6.8 %collective-permute-start.24 = (f32[32,16,2]{2,1,0:T(8,128)S(1)}, f32[32,16,2]{2,1,0:T(8,128)S(1)}, u32[]{:S(2)}, u32[]{:S(2)}) collective-permute-start(f32[32,16,2]{2,1,0:T(8,128)S(1)} %get-tuple-element.51), channel_id=1, source_target_pairs={{0,16},{1,17},{2,18},{3,19},{4,20},{5,21},{6,22},{7,23},{8,24},{9,... | collective-permute-start | bytes 12296 | tf_op jit(solution)/shard_map/ppermute | solution.py:21
  103.0 10.1 %collective-permute-start.25 = (f32[32,16,2]{2,1,0:T(8,128)S(1)}, f32[32,16,2]{2,1,0:T(8,128)S(1)}, u32[]{:S(2)}, u32[]{:S(2)}) collective-permute-start(f32[32,16,2]{2,1,0:T(8,128)S(1)} %get-tuple-element.52), channel_id=1, source_target_pairs={{16,0},{17,1},{18,2},{19,3},{20,4},{21,5},{22,6},{23,7},{24,8},{25... | collective-permute-start | bytes 12296 | tf_op jit(solution)/shard_map/ppermute | solution.py:22
  113.3 4.0 %collective-permute-start.26 = (f32[32,2,132]{2,1,0:T(2,128)S(1)}, f32[32,2,132]{2,1,0:T(2,128)S(1)}, u32[]{:S(2)}, u32[]{:S(2)}) collective-permute-start(f32[32,2,132]{2,1,0:T(2,128)S(1)} %get-tuple-element.37), channel_id=1, source_target_pairs={{0,4},{4,8},{8,12},{1,5},{5,9},{9,13},{2,6},{6,10},{10,14},{3,7},{... | collective-permute-start | bytes 101384 | tf_op jit(solution)/shard_map/ppermute | solution.py:21
  116.1 3.4 %collective-permute-start.27 = (f32[32,2,132]{2,1,0:T(2,128)S(1)}, f32[32,2,132]{2,1,0:T(2,128)S(1)}, u32[]{:S(2)}, u32[]{:S(2)}) collective-permute-start(f32[32,2,132]{2,1,0:T(2,128)S(1)} %get-tuple-element.38), channel_id=1, source_target_pairs={{4,0},{8,4},{12,8},{5,1},{9,5},{13,9},{6,2},{10,6},{14,10},{7,3},{... | collective-permute-start | bytes 101384 | tf_op jit(solution)/shard_map/ppermute | solution.py:22
  119.6 5.2 %collective-permute-start.28 = (f32[2,20,132]{2,1,0:T(8,128)S(1)}, f32[2,20,132]{2,1,0:T(8,128)S(1)}, u32[]{:S(2)}, u32[]{:S(2)}) collective-permute-start(f32[2,20,132]{2,1,0:T(8,128)S(1)} %get-tuple-element.29), channel_id=1, source_target_pairs={{0,1},{1,2},{2,3},{4,5},{5,6},{6,7},{8,9},{9,10},{10,11},{12,13},{... | collective-permute-start | bytes 63368 | tf_op jit(solution)/shard_map/ppermute | solution.py:21
  123.1 6.0 %collective-permute-start.29 = (f32[2,20,132]{2,1,0:T(8,128)S(1)}, f32[2,20,132]{2,1,0:T(8,128)S(1)}, u32[]{:S(2)}, u32[]{:S(2)}) collective-permute-start(f32[2,20,132]{2,1,0:T(8,128)S(1)} %get-tuple-element.30), channel_id=1, source_target_pairs={{1,0},{2,1},{3,2},{5,4},{6,5},{7,6},{9,8},{10,9},{11,10},{13,12},{... | collective-permute-start | bytes 63368 | tf_op jit(solution)/shard_map/ppermute | solution.py:22
  175.3 37.2 %copy-start.3 = (f32[32,16,128]{2,1,0:T(8,128)}, f32[32,16,128]{2,1,0:T(8,128)S(1)}, u32[]{:S(2)}) copy-start(f32[32,16,128]{2,1,0:T(8,128)S(1)} %multiply_subtract_fusion.1) | copy-start | bytes 786436
  175.5 9.7 %collective-permute-start.30 = (f32[32,16,4]{2,1,0:T(8,128)S(1)}, f32[32,16,4]{2,1,0:T(8,128)S(1)}, u32[]{:S(2)}, u32[]{:S(2)}) collective-permute-start(f32[32,16,4]{2,1,0:T(8,128)S(1)} %get-tuple-element.49), channel_id=1, source_target_pairs={{0,16},{1,17},{2,18},{3,19},{4,20},{5,21},{6,22},{7,23},{8,24},{9,... | collective-permute-start | bytes 24584 | tf_op jit(solution)/shard_map/ppermute | solution.py:21
  180.0 9.3 %collective-permute-start.31 = (f32[32,16,4]{2,1,0:T(8,128)S(1)}, f32[32,16,4]{2,1,0:T(8,128)S(1)}, u32[]{:S(2)}, u32[]{:S(2)}) collective-permute-start(f32[32,16,4]{2,1,0:T(8,128)S(1)} %get-tuple-element.50), channel_id=1, source_target_pairs={{16,0},{17,1},{18,2},{19,3},{20,4},{21,5},{22,6},{23,7},{24,8},{25... | collective-permute-start | bytes 24584 | tf_op jit(solution)/shard_map/ppermute | solution.py:22
  189.5 2.6 collective-permute-start.32
  190.8 4.3 %collective-permute-start.33 = (f32[32,4,136]{2,1,0:T(4,128)S(1)}, f32[32,4,136]{2,1,0:T(4,128)S(1)}, u32[]{:S(2)}, u32[]{:S(2)}) collective-permute-start(f32[32,4,136]{2,1,0:T(4,128)S(1)} %get-tuple-element.36), channel_id=1, source_target_pairs={{4,0},{8,4},{12,8},{5,1},{9,5},{13,9},{6,2},{10,6},{14,10},{7,3},{... | collective-permute-start | bytes 208904 | tf_op jit(solution)/shard_map/ppermute | solution.py:22
  195.3 6.1 %collective-permute-start.34 = (f32[4,24,136]{2,1,0:T(8,128)S(1)}, f32[4,24,136]{2,1,0:T(8,128)S(1)}, u32[]{:S(2)}, u32[]{:S(2)}) collective-permute-start(f32[4,24,136]{2,1,0:T(8,128)S(1)} %get-tuple-element.23), channel_id=1, source_target_pairs={{0,1},{1,2},{2,3},{4,5},{5,6},{6,7},{8,9},{9,10},{10,11},{12,13},{... | collective-permute-start | bytes 156680 | tf_op jit(solution)/shard_map/ppermute | solution.py:21
  199.3 6.5 %collective-permute-start.35 = (f32[4,24,136]{2,1,0:T(8,128)S(1)}, f32[4,24,136]{2,1,0:T(8,128)S(1)}, u32[]{:S(2)}, u32[]{:S(2)}) collective-permute-start(f32[4,24,136]{2,1,0:T(8,128)S(1)} %get-tuple-element.24), channel_id=1, source_target_pairs={{1,0},{2,1},{3,2},{5,4},{6,5},{7,6},{9,8},{10,9},{11,10},{13,12},{... | collective-permute-start | bytes 156680 | tf_op jit(solution)/shard_map/ppermute | solution.py:22
  256.6 32.0 %copy-start.2 = (f32[32,16,128]{2,1,0:T(8,128)}, f32[32,16,128]{2,1,0:T(8,128)S(1)}, u32[]{:S(2)}) copy-start(f32[32,16,128]{2,1,0:T(8,128)S(1)} %multiply_add_fusion.1) | copy-start | bytes 786436
  256.7 9.6 %collective-permute-start.36 = (f32[32,16,2]{2,1,0:T(8,128)S(1)}, f32[32,16,2]{2,1,0:T(8,128)S(1)}, u32[]{:S(2)}, u32[]{:S(2)}) collective-permute-start(f32[32,16,2]{2,1,0:T(8,128)S(1)} %get-tuple-element.47), channel_id=1, source_target_pairs={{0,16},{1,17},{2,18},{3,19},{4,20},{5,21},{6,22},{7,23},{8,24},{9,... | collective-permute-start | bytes 12296 | tf_op jit(solution)/shard_map/ppermute | solution.py:21
  261.1 9.4 %collective-permute-start.37 = (f32[32,16,2]{2,1,0:T(8,128)S(1)}, f32[32,16,2]{2,1,0:T(8,128)S(1)}, u32[]{:S(2)}, u32[]{:S(2)}) collective-permute-start(f32[32,16,2]{2,1,0:T(8,128)S(1)} %get-tuple-element.48), channel_id=1, source_target_pairs={{16,0},{17,1},{18,2},{19,3},{20,4},{21,5},{22,6},{23,7},{24,8},{25... | collective-permute-start | bytes 12296 | tf_op jit(solution)/shard_map/ppermute | solution.py:22
  270.7 2.6 collective-permute-start.38
  272.0 4.3 %collective-permute-start.39 = (f32[32,2,132]{2,1,0:T(2,128)S(1)}, f32[32,2,132]{2,1,0:T(2,128)S(1)}, u32[]{:S(2)}, u32[]{:S(2)}) collective-permute-start(f32[32,2,132]{2,1,0:T(2,128)S(1)} %get-tuple-element.34), channel_id=1, source_target_pairs={{4,0},{8,4},{12,8},{5,1},{9,5},{13,9},{6,2},{10,6},{14,10},{7,3},{... | collective-permute-start | bytes 101384 | tf_op jit(solution)/shard_map/ppermute | solution.py:22
  276.4 5.0 %collective-permute-start.40 = (f32[2,20,132]{2,1,0:T(8,128)S(1)}, f32[2,20,132]{2,1,0:T(8,128)S(1)}, u32[]{:S(2)}, u32[]{:S(2)}) collective-permute-start(f32[2,20,132]{2,1,0:T(8,128)S(1)} %get-tuple-element.27), channel_id=1, source_target_pairs={{0,1},{1,2},{2,3},{4,5},{5,6},{6,7},{8,9},{9,10},{10,11},{12,13},{... | collective-permute-start | bytes 63368 | tf_op jit(solution)/shard_map/ppermute | solution.py:21
  279.7 6.0 %collective-permute-start.41 = (f32[2,20,132]{2,1,0:T(8,128)S(1)}, f32[2,20,132]{2,1,0:T(8,128)S(1)}, u32[]{:S(2)}, u32[]{:S(2)}) collective-permute-start(f32[2,20,132]{2,1,0:T(8,128)S(1)} %get-tuple-element.28), channel_id=1, source_target_pairs={{1,0},{2,1},{3,2},{5,4},{6,5},{7,6},{9,8},{10,9},{11,10},{13,12},{... | collective-permute-start | bytes 63368 | tf_op jit(solution)/shard_map/ppermute | solution.py:22
  288.6 41.8 %copy-start.4 = (f32[32,16,128]{2,1,0:T(8,128)S(1)}, f32[32,16,128]{2,1,0:T(8,128)}, u32[]{:S(2)}) copy-start(f32[32,16,128]{2,1,0:T(8,128)} %copy-done.3) | copy-start | bytes 786436
  288.6 41.8 %copy-start.6 = (f32[32,16,128]{2,1,0:T(8,128)S(1)}, f32[32,16,128]{2,1,0:T(8,128)}, u32[]{:S(2)}) copy-start(f32[32,16,128]{2,1,0:T(8,128)} %param.4) | copy-start | bytes 786436
where the time goes:
time: 334 us; the launch traced here: 332 us
  blocking collectives  118 us (35%)
  starting transfers between devices  97.9 us (29%)
  waiting for transfers between devices  73.6 us (22%)
  other arithmetic  36.1 us (11%)
  between operations  5.47 us (2%)
    psum x3, blocking collectives, global_dot(): return lax.psum(jnp.sum(first_field * second_field), ('gx', 'gy', 'gz'))  118 us
    ppermute x21, starting transfers between devices, padded_2(): before = lax.ppermute(last, axis, up)  70.3 us
    ppermute x21, waiting for transfers between devices, padded_2(): after = lax.ppermute(first, axis, down)  52.6 us
    ppermute x21, starting transfers between devices, padded_2(): after = lax.ppermute(first, axis, down)  27.6 us
    ppermute x21, waiting for transfers between devices, padded_2(): before = lax.ppermute(last, axis, up)  21 us
    mul x7, other arithmetic, k_box(): ((6.0 + coef_box) * crop_box(padded, 1) - neighbours(padded)) / 6.0  15.3 us
  transfers between devices with their start and end apart: 42, of which 24 were waited for; matrix products, arithmetic and copies ran while one was open for 1% of the time, Pallas kernels for 0%

commit v1 on v0

v1 whole, which is shorter than its diff:
```python
import functools
import jax
import jax.numpy as jnp
from jax import lax
from jax.experimental import pallas as pl
from jax.experimental.pallas import tpu as pltpu
from jax.sharding import PartitionSpec as P

SWEEPS = 3
cheb_high = 7.2
cheb_low = 0.072
MESH = pl.DeviceIdType.MESH
AXES = ("gx", "gy", "gz")


def sweep_weights():
    centre = (cheb_high + cheb_low) / 2.0
    half_width = (cheb_high - cheb_low) / 2.0
    sigma = centre / half_width
    old = 1.0 / sigma
    weights = []
    for _ in range(SWEEPS - 1):
        new = 1.0 / (2.0 * sigma - old)
        weights.append((new * old, 2.0 * new / half_width))
        old = new
    return 1.0 / centre, weights


def kernel(sizes, shape, b_ref, x0_ref, kap_ref, x_ref, r_ref,
           v_ref, u_ref, t_ref, c_ref, r0_ref, z0_ref, a0_ref, d_ref,
           xsend, ysend, xhalo, yhalo, zhalo, part, gather_x, gather_y, gather_z,
           send_sem, recv_sem, red_send, red_recv):
    Z, Y, X = shape
    N = Z * Y
    CH = min(N, 8 * Y)
    chunks = [(i, CH) for i in range(0, N, CH)]
    me = {a: lax.axis_index(a) for a in AXES}
    inv_centre, weights = sweep_weights()
    inv36 = 1.0 / 36.0

    xhalo[...] = jnp.zeros_like(xhalo)
    yhalo[...] = jnp.zeros_like(yhalo)
    zhalo[...] = jnp.zeros_like(zhalo)

    barrier = pltpu.get_barrier_semaphore()
    count = 0
    for a in AXES:
        for k in range(1, sizes[a]):
            peer = lax.rem(me[a] + k, sizes[a])
            pl.semaphore_signal(barrier, inc=1, device_id={a: peer}, device_id_type=MESH)
            count += 1

    for ref in (v_ref, u_ref):
        ref[0:Y, :] = jnp.zeros((Y, X), jnp.float32)
        ref[Y + N:2 * Y + N, :] = jnp.zeros((Y, X), jnp.float32)
    for i, n in chunks:
        v_ref[Y + i:Y + i + n, :] = x0_ref[i:i + n, :]
        c_ref[i:i + n, :] = 6.0 + kap_ref[i:i + n, :]

    lane_y = lax.broadcasted_iota(jnp.int32, (Y, X), 1)
    half_y = lane_y // 2
    even_y = lane_y % 2 == 0
    edge_y = (lane_y == 0) | (lane_y == X - 1)
    lane_c = lax.broadcasted_iota(jnp.int32, (CH, X), 1)
    row_c = lax.broadcasted_iota(jnp.int32, (CH, X), 0) % Y
    first_x, last_x = lane_c == 0, lane_c == X - 1
    first_y, last_y = row_c == 0, row_c == Y - 1

    pl.semaphore_wait(barrier, count)

    def has(a, side):
        return me[a] > 0 if side == 0 else me[a] < sizes[a] - 1

    def halo_copy(src_ref, slot, ai, side, halo_side):
        a = AXES[ai]
        if ai == 0:
            src, halo = xsend.at[slot], xhalo
        elif ai == 1:
            src, halo = ysend.at[slot, side], yhalo
        else:
            src, halo = src_ref.at[pl.ds(Y if side == 0 else N, Y)], zhalo
        return pltpu.make_async_remote_copy(
            src_ref=src, dst_ref=halo.at[slot, halo_side],
            send_sem=send_sem.at[slot, ai, side],
            recv_sem=recv_sem.at[slot, ai, halo_side],
            device_id={a: me[a] + (2 * side - 1)}, device_id_type=MESH)

    def each_side(order, fn):
        for ai in order:
            if sizes[AXES[ai]] > 1:
                for side in (0, 1):
                    pl.when(has(AXES[ai], side))(functools.partial(fn, ai, side))

    def k_step(step, src, dst, dst_off, post, middle=None):
        slot = step % 2

        def start(ai, side):
            halo_copy(src, slot, ai, side, 1 - side).start()

        def finish(ai, side):
            halo_copy(src, slot, ai, side, side).wait_recv()
            halo_copy(src, slot, ai, side, 1 - side).wait_send()

        each_side((2,), start)
        for side, row in ((0, 0), (1, Y - 1)):
            ysend[slot, side] = src[pl.ds(Y + row, Z, stride=Y), :]
        each_side((1,), start)
        acc = jnp.zeros((Y, X), jnp.float32)
        for k in range(Z):
            v = src[Y + k * Y:2 * Y + k * Y, :]
            acc = jnp.where(half_y == k, pltpu.roll(v, (1 + 2 * k) % X, 1), acc)
        xsend[slot] = acc
        each_side((0,), start)

        for i, n in chunks:
            v = src[Y + i:Y + i + n, :]
            total = src[i:i + n, :] + src[2 * Y + i:2 * Y + i + n, :]
            total = total + jnp.where(first_x, 0.0, pltpu.roll(v, 1, 1))
            total = total + jnp.where(last_x, 0.0, pltpu.roll(v, X - 1, 1))
            total = total + jnp.where(first_y, 0.0, pltpu.roll(v, 1, 0))
            total = total + jnp.where(last_y, 0.0, pltpu.roll(v, n - 1, 0))
            dst[dst_off + i:dst_off + i + n, :] = c_ref[i:i + n, :] * v - total
        if middle is not None:
            middle()

        each_side((2, 1, 0), finish)
        for side, row in ((0, 0), (1, N - Y)):
            rows = slice(dst_off + row, dst_off + row + Y)
            dst[rows, :] = dst[rows, :] - zhalo[slot, side]
        for side, row in ((0, 0), (1, Y - 1)):
            rows = pl.ds(dst_off + row, Z, stride=Y)
            dst[rows, :] = dst[rows, :] - yhalo[slot, side]
        pairs = jnp.where(even_y, pltpu.roll(xhalo[slot, 1], X - 1, 1),
                          pltpu.roll(xhalo[slot, 0], 1, 1))
        for k in range(Z):
            rows = slice(dst_off + k * Y, dst_off + (k + 1) * Y)
            fix = jnp.where(edge_y, pltpu.roll(pairs, (X - 1 - 2 * k) % X, 1), 0.0)
            post(k * Y, dst[rows, :] - fix)

    def store_u(i, value):
        u_ref[Y + i:2 * Y + i, :] = value

    def q_step(step, post):
        k_step(step, v_ref, u_ref, Y, store_u)
        k_step(step + 1, u_ref, t_ref, 0, post)

    def post_residual(i, t):
        rows = slice(i, i + Y)
        res = b_ref[rows, :] - t * inv36
        r0_ref[rows, :] = res
        upd = res * inv_centre
        d_ref[rows, :] = upd
        v_ref[Y + i:2 * Y + i, :] = upd

    def post_sweep(source, weight_old, weight_new, i, t, sink=None):
        rows = slice(i, i + Y)
        src = source[rows, :]
        upd = weight_old * d_ref[rows, :] + weight_new * (src - t * inv36)
        d_ref[rows, :] = upd
        z = v_ref[Y + i:2 * Y + i, :] + upd
        v_ref[Y + i:2 * Y + i, :] = z
        if sink is not None:
            sink(rows, src, z)

    sums = {}

    def add(name, value):
        sums[name] = value if name not in sums else sums[name] + value

    step = 0
    q_step(step, post_residual)
    step += 2

    def sink_z0(rows, src, z):
        z0_ref[rows, :] = z
        add("e0", src * z)

    def sink_w(rows, src, z):
        add("g2", src * z)

    def sweeps(step, source, sink):
        for j, (wo, wn) in enumerate(weights):
            last = sink if j + 1 == len(weights) else None
            q_step(step, functools.partial(post_sweep, source, wo, wn, sink=last))
            step += 2
        return step

    step = sweeps(step, r0_ref, sink_z0)

    def post_applied(i, t):
        rows = slice(i, i + Y)
        a0 = t * inv36
        a0_ref[rows, :] = a0
        add("g1", z0_ref[rows, :] * a0)
        upd = a0 * inv_centre
        d_ref[rows, :] = upd
        v_ref[Y + i:2 * Y + i, :] = upd

    q_step(step, post_applied)
    step += 2
    step = sweeps(step, a0_ref, sink_w)

    def post_u(i, value):
        store_u(i, value)
        add("g3", value * value)

    k_step(step, v_ref, u_ref, Y, post_u)

    gathers = {"gx": gather_x, "gy": gather_y, "gz": gather_z}

    def red_copy(ai, k, slot):
        a = AXES[ai]
        peer = lax.rem(me[a] + k, sizes[a])
        return pltpu.make_async_remote_copy(
            src_ref=part.at[ai], dst_ref=gathers[a].at[slot],
            send_sem=red_send.at[ai, k], recv_sem=red_recv.at[ai, k],
            device_id={a: peer}, device_id_type=MESH)

    def red_start(ai, value):
        a = AXES[ai]
        part[ai] = value
        gathers[a][pl.ds(me[a], 1)] = value[None]
        for k in range(1, sizes[a]):
            red_copy(ai, k, me[a]).start()

    def red_finish(ai):
        a = AXES[ai]
        for k in range(1, sizes[a]):
            red_copy(ai, k, lax.rem(me[a] + sizes[a] - k, sizes[a])).wait_recv()
            red_copy(ai, k, me[a]).wait_send()
        total = gathers[a][0]
        for j in range(1, sizes[a]):
            total = total + gathers[a][j]
        return total

    rows8 = lax.broadcasted_iota(jnp.int32, (8, X), 0)
    mine = jnp.zeros((8, X), jnp.float32)
    for j, name in enumerate(("e0", "g1", "g2", "g3")):
        mine = jnp.where(rows8 == j, jnp.sum(sums[name], axis=0, keepdims=True), mine)
    red_start(1, mine)

    def middle():
        red_start(0, red_finish(1))

    def post_qw(i, t):
        t_ref[i:i + Y, :] = t

    k_step(step + 1, u_ref, t_ref, 0, post_qw, middle)
    red_start(2, red_finish(0))
    totals = jnp.sum(red_finish(2), axis=1, keepdims=True)
    e0, g1, g2 = totals[0:1], totals[1:2], totals[2:3]
    g3 = totals[3:4] * inv36
    alpha = e0 / g1
    e1 = e0 - 2.0 * alpha * g1 + alpha * alpha * g2
    keep = 1.0 + e1 / e0
    den = keep * keep * g1 - 2.0 * keep * alpha * g2 + alpha * alpha * g3
    alpha1 = e1 / den
    p = alpha + alpha1 * keep
    q = alpha1 * alpha
    q36 = q * inv36
    for i, n in chunks:
        rows = slice(i, i + n)
        x_ref[rows, :] = x0_ref[rows, :] + p * z0_ref[rows, :] - q * v_ref[Y + i:Y + i + n, :]
        r_ref[rows, :] = r0_ref[rows, :] - p * a0_ref[rows, :] + q36 * t_ref[rows, :]


def body(sizes, right_side, initial, kappa_sq):
    Z, Y, X = right_side.shape
    N = Z * Y
    f32 = jnp.float32
    flat = lambda a: a.reshape(N, X)
    vm = pl.BlockSpec(memory_space=pltpu.VMEM)
    big = max(sizes.values())
    out = pl.pallas_call(
        functools.partial(kernel, sizes, (Z, Y, X)),
        out_shape=[jax.ShapeDtypeStruct((N, X), f32)] * 2,
        in_specs=[vm] * 3,
        out_specs=[vm] * 2,
        scratch_shapes=[
            pltpu.VMEM((N + 2 * Y, X), f32),
            pltpu.VMEM((N + 2 * Y, X), f32),
        ] + [pltpu.VMEM((N, X), f32)] * 6 + [
            pltpu.VMEM((2, Y, X), f32),
            pltpu.VMEM((2, 2, Z, X), f32),
            pltpu.VMEM((2, 2, Y, X), f32),
            pltpu.VMEM((2, 2, Z, X), f32),
            pltpu.VMEM((2, 2, Y, X), f32),
            pltpu.VMEM((3, 8, X), f32),
        ] + [pltpu.VMEM((sizes[a], 8, X), f32) for a in AXES] + [
            pltpu.SemaphoreType.DMA((2, 3, 2)),
            pltpu.SemaphoreType.DMA((2, 3, 2)),
            pltpu.SemaphoreType.DMA((3, big)),
            pltpu.SemaphoreType.DMA((3, big)),
        ],
        compiler_params=pltpu.CompilerParams(
            collective_id=0, has_side_effects=True, vmem_limit_bytes=24 * 1024 * 1024),
        name="cg",
    )(flat(right_side), flat(initial), flat(kappa_sq))
    return tuple(o.reshape(Z, Y, X) for o in out)


def solution(mesh):
    spec = P("gz", "gy", "gx")
    sizes = {a: mesh.shape[a] for a in AXES}
    return jax.shard_map(functools.partial(body, sizes), mesh=mesh, in_specs=(spec,) * 3,
                         out_specs=(spec,) * 2, check_vma=False)
```

time: 334 us -> 59.2 us (0.18)
  blocking collectives: 118 us -> 0 us
  starting transfers between devices: 97.9 us -> 0 us
  waiting for transfers between devices: 73.6 us -> 0 us
  Pallas kernels: 0 us -> 54.1 us
  other arithmetic: 36.1 us -> 0 us
  between operations: 5.47 us -> 0.65 us
    psum x3 -> x0, blocking collectives: 118 us -> none  [global_dot(): return lax.psum(jnp.sum(first_field * second_field), ('gx', 'gy', 'gz'))]
    ppermute x42 -> x0, starting transfers between devices: 97.9 us -> none  [the longest x21 70.3 us: padded_2(): before = lax.ppermute(last, axis, up)]
    ppermute x42 -> x0, waiting for transfers between devices: 73.6 us -> none  [the longest x21 52.6 us: padded_2(): after = lax.ppermute(first, axis, down)]
    pallas_call x0 -> x1, Pallas kernels: none -> 54.1 us  [body(): pl.pallas_call(functools.partial(kernel, sizes, (Z, Y, X)), out_shape=[ja...]
    mul x9 -> x0, other arithmetic: 15.6 us -> none  [the longest x7 15.3 us: k_box(): ((6.0 + coef_box) * crop_box(padded, 1) - neighbours(padded)) / 6.0]
    add x4 -> x0, other arithmetic: 6.5 us -> none  [the longest x3 5.51 us: precondition_box(): result = result + update]
    reduce_sum x3 -> x0, other arithmetic: 5.02 us -> none  [global_dot(): return lax.psum(jnp.sum(first_field * second_field), ('gx', 'gy', 'gz'))]
    unnamed x16 -> x8, local copies, waits for them, and re-layouts: 0.05 us -> 4.25 us
  transfers between devices with their start and end apart: 42 -> 0, of which waited for: 24 -> 0; matrix products, arithmetic and copies ran while one was open for 1% -> 0% of each run, Pallas kernels for 0% -> 0%
where the time goes in v1:
time: 59.2 us; the launch traced here: 59 us
  Pallas kernels  54.1 us (91%)
  local copies, waits for them, and re-layouts  4.25 us (7%)
  between operations  0.65 us (1%)
    pallas_call x1, Pallas kernels, body(): pl.pallas_call(functools.partial(kernel, sizes, (Z, Y, X)), out_shape=[ja...  54.1 us
    unnamed x8, local copies, waits for them, and re-layouts  4.25 us

profile of v1, /device:TPU:0, one launch (start us, length us, event | category | flops | bytes accessed | tf_op | source)
XLA Modules:
  0.0 59.0 jit_solution(7588917415486327001)
XLA Ops:
  0.6 0.0 copy-start
  0.6 0.9 %copy-done = f32[32,16,128]{2,1,0:T(8,128)S(1)} copy-done((f32[32,16,128]{2,1,0:T(8,128)S(1)}, f32[32,16,128]{2,1,0:T(8,128)}, u32[]{:S(2)}) %copy-start) | copy-done | bytes 262168
  1.6 0.0 copy-start.1
  1.6 0.9 %copy-done.1 = f32[32,16,128]{2,1,0:T(8,128)S(1)} copy-done((f32[32,16,128]{2,1,0:T(8,128)S(1)}, f32[32,16,128]{2,1,0:T(8,128)}, u32[]{:S(2)}) %copy-start.1) | copy-done | bytes 262168
  2.5 0.0 copy-start.2
  2.5 0.9 %copy-done.2 = f32[32,16,128]{2,1,0:T(8,128)S(1)} copy-done((f32[32,16,128]{2,1,0:T(8,128)S(1)}, f32[32,16,128]{2,1,0:T(8,128)}, u32[]{:S(2)}) %copy-start.2) | copy-done | bytes 262168
  3.5 54.1 %cg.1 = (f32[512,128]{1,0:T(8,128)S(1)}, f32[512,128]{1,0:T(8,128)S(1)}) custom-call(f32[512,128]{1,0:T(8,128)S(1)} %bitcast.5, f32[512,128]{1,0:T(8,128)S(1)} %bitcast.6, f32[512,128]{1,0:T(8,128)S(1)} %bitcast.7), custom_call_target="tpu_custom_call" | custom-call | tf_op jit(solution)/shard_map/cg/pallas_call | solution.py:274
  57.6 0.7 %copy.7 = f32[32,16,128]{2,1,0:T(8,128)} copy(f32[32,16,128]{2,1,0:T(8,128)S(1)} %bitcast.9) | data formatting | bytes 524288
  58.3 0.7 %copy.8 = f32[32,16,128]{2,1,0:T(8,128)} copy(f32[32,16,128]{2,1,0:T(8,128)S(1)} %bitcast.8) | data formatting | bytes 524288
Async XLA Ops:
  0.6 1.0 %copy-start = (f32[32,16,128]{2,1,0:T(8,128)S(1)}, f32[32,16,128]{2,1,0:T(8,128)}, u32[]{:S(2)}) copy-start(f32[32,16,128]{2,1,0:T(8,128)} %param.3) | copy-start | bytes 786436
  1.6 0.9 %copy-start.1 = (f32[32,16,128]{2,1,0:T(8,128)S(1)}, f32[32,16,128]{2,1,0:T(8,128)}, u32[]{:S(2)}) copy-start(f32[32,16,128]{2,1,0:T(8,128)} %param.4) | copy-start | bytes 786436
  2.5 0.9 %copy-start.2 = (f32[32,16,128]{2,1,0:T(8,128)S(1)}, f32[32,16,128]{2,1,0:T(8,128)}, u32[]{:S(2)}) copy-start(f32[32,16,128]{2,1,0:T(8,128)} %param.5) | copy-start | bytes 786436

commit v2 on v1

v2 whole, which is shorter than its diff:
```python
import functools
import jax
import jax.numpy as jnp
from jax import lax
from jax.experimental import pallas as pl
from jax.experimental.pallas import tpu as pltpu
from jax.sharding import PartitionSpec as P

SWEEPS = 3
cheb_high = 7.2
cheb_low = 0.072
MESH = pl.DeviceIdType.MESH
AXES = ("gx", "gy", "gz")


def sweep_weights():
    centre = (cheb_high + cheb_low) / 2.0
    half_width = (cheb_high - cheb_low) / 2.0
    sigma = centre / half_width
    old = 1.0 / sigma
    weights = []
    for _ in range(SWEEPS - 1):
        new = 1.0 / (2.0 * sigma - old)
        weights.append((new * old, 2.0 * new / half_width))
        old = new
    return 1.0 / centre, weights


def kernel(sizes, shape, b_hbm, x0_hbm, kap_hbm, x_ref, r_ref,
           v_ref, e_ref, u_ref, t_ref, c_ref, d_ref,
           xsend, ysend, xhalo, yhalo, zhalo, sums_s, sums_v, sums_u, part,
           gather_x, gather_y, gather_z,
           send_sem, recv_sem, red_send, red_recv, in_sem):
    Z, Y, X = shape
    N = Z * Y
    me = {a: lax.axis_index(a) for a in AXES}
    inv_centre, weights = sweep_weights()
    inv36 = 1.0 / 36.0
    half = SWEEPS
    last_q = 2 * half
    zero_slot = last_q + 2

    loads = [pltpu.make_async_copy(x0_hbm, v_ref.at[0, pl.ds(Y, N)], in_sem.at[0]),
             pltpu.make_async_copy(kap_hbm, c_ref, in_sem.at[1]),
             pltpu.make_async_copy(b_hbm, e_ref.at[0], in_sem.at[2])]
    for load in loads:
        load.start()

    xhalo[...] = jnp.zeros_like(xhalo)
    yhalo[...] = jnp.zeros_like(yhalo)
    zhalo[...] = jnp.zeros_like(zhalo)

    barrier = pltpu.get_barrier_semaphore()
    count = 0
    for a in AXES:
        for k in range(1, sizes[a]):
            peer = lax.rem(me[a] + k, sizes[a])
            pl.semaphore_signal(barrier, inc=1, device_id={a: peer}, device_id_type=MESH)
            count += 1

    guard = jnp.zeros((Y, X), jnp.float32)
    for j in range(last_q + 2):
        v_ref[j, 0:Y, :] = guard
        v_ref[j, Y + N:2 * Y + N, :] = guard
    u_ref[0:Y, :] = guard
    u_ref[Y + N:2 * Y + N, :] = guard
    for k in range(Z):
        e_ref[zero_slot, k * Y:(k + 1) * Y, :] = guard
        d_ref[k * Y:(k + 1) * Y, :] = guard

    lane = lax.broadcasted_iota(jnp.int32, (Y, X), 1)
    row = lax.broadcasted_iota(jnp.int32, (Y, X), 0)
    half_lane = lane // 2
    even = lane % 2 == 0
    first_x, last_x = lane == 0, lane == X - 1
    edge_x = first_x | last_x
    first_y, last_y = row == 0, row == Y - 1

    loads[0].wait()
    loads[1].wait()
    for k in range(Z):
        rows = slice(k * Y, (k + 1) * Y)
        c_ref[rows, :] = 6.0 + c_ref[rows, :]
    loads[2].wait()
    pl.semaphore_wait(barrier, count)

    def has(a, side):
        return me[a] > 0 if side == 0 else me[a] < sizes[a] - 1

    def halo_copy(src_ref, slot, ai, side, halo_side):
        a = AXES[ai]
        if ai == 0:
            src, halo = xsend.at[slot], xhalo
        elif ai == 1:
            src, halo = ysend.at[slot, side], yhalo
        else:
            src, halo = src_ref.at[pl.ds(Y if side == 0 else N, Y)], zhalo
        return pltpu.make_async_remote_copy(
            src_ref=src, dst_ref=halo.at[slot, halo_side],
            send_sem=send_sem.at[slot, ai, side],
            recv_sem=recv_sem.at[slot, ai, halo_side],
            device_id={a: me[a] + (2 * side - 1)}, device_id_type=MESH)

    def each_side(order, fn):
        for ai in order:
            if sizes[AXES[ai]] > 1:
                for side in (0, 1):
                    pl.when(has(AXES[ai], side))(functools.partial(fn, ai, side))

    def k_step(slot, src, dst, dst_off, post, middle=None):
        def start(ai, side):
            halo_copy(src, slot, ai, side, 1 - side).start()

        def finish(ai, side):
            halo_copy(src, slot, ai, side, side).wait_recv()
            halo_copy(src, slot, ai, side, 1 - side).wait_send()

        each_side((2,), start)
        for side, first in ((0, 0), (1, Y - 1)):
            ysend[slot, side] = src[pl.ds(Y + first, Z, stride=Y), :]
        each_side((1,), start)
        acc = jnp.zeros((Y, X), jnp.float32)
        for k in range(Z):
            v = src[Y + k * Y:2 * Y + k * Y, :]
            acc = jnp.where(half_lane == k, pltpu.roll(v, (1 + 2 * k) % X, 1), acc)
        xsend[slot] = acc
        each_side((0,), start)

        for k in range(Z):
            i = Y + k * Y
            v = src[i:i + Y, :]
            total = src[i - Y:i, :] + src[i + Y:i + 2 * Y, :]
            total = total + jnp.where(first_x, 0.0, pltpu.roll(v, 1, 1))
            total = total + jnp.where(last_x, 0.0, pltpu.roll(v, X - 1, 1))
            total = total + jnp.where(first_y, 0.0, src[i - 1:i - 1 + Y, :])
            total = total + jnp.where(last_y, 0.0, src[i + 1:i + 1 + Y, :])
            dst[dst_off + k * Y:dst_off + (k + 1) * Y, :] = c_ref[k * Y:(k + 1) * Y, :] * v - total
        if middle is not None:
            middle()

        each_side((2, 1, 0), finish)
        for side, first in ((0, 0), (1, N - Y)):
            rows = slice(dst_off + first, dst_off + first + Y)
            dst[rows, :] = dst[rows, :] - zhalo[slot, side]
        for side, first in ((0, 0), (1, Y - 1)):
            rows = pl.ds(dst_off + first, Z, stride=Y)
            dst[rows, :] = dst[rows, :] - yhalo[slot, side]
        pairs = jnp.where(even, pltpu.roll(xhalo[slot, 1], X - 1, 1),
                          pltpu.roll(xhalo[slot, 0], 1, 1))
        for k in range(Z):
            rows = slice(dst_off + k * Y, dst_off + (k + 1) * Y)
            fix = jnp.where(edge_x, pltpu.roll(pairs, (X - 1 - 2 * k) % X, 1), 0.0)
            post(k, dst[rows, :] - fix)

    gathers = {"gx": gather_x, "gy": gather_y, "gz": gather_z}

    def red_copy(ai, k, slot):
        a = AXES[ai]
        peer = lax.rem(me[a] + k, sizes[a])
        return pltpu.make_async_remote_copy(
            src_ref=part.at[ai], dst_ref=gathers[a].at[slot],
            send_sem=red_send.at[ai, k], recv_sem=red_recv.at[ai, k],
            device_id={a: peer}, device_id_type=MESH)

    def red_start(ai, value):
        a = AXES[ai]
        part[ai] = value
        gathers[a][pl.ds(me[a], 1)] = value[None]
        for k in range(1, sizes[a]):
            red_copy(ai, k, me[a]).start()

    def red_finish(ai):
        a = AXES[ai]
        for k in range(1, sizes[a]):
            red_copy(ai, k, lax.rem(me[a] + sizes[a] - k, sizes[a])).wait_recv()
            red_copy(ai, k, me[a]).wait_send()
        total = gathers[a][0]
        for j in range(1, sizes[a]):
            total = total + gathers[a][j]
        return total

    def red_first():
        rows8 = lax.broadcasted_iota(jnp.int32, (8, X), 0)
        mine = jnp.zeros((8, X), jnp.float32)
        for j, value in enumerate((sums_s[half - 1], sums_v[half], sums_s[last_q - 1], sums_u[...])):
            mine = jnp.where(rows8 == j, jnp.sum(value, axis=0, keepdims=True), mine)
        red_start(1, mine)

    def red_second():
        red_start(0, red_finish(1))

    def q_body(q, carry):
        phase = lax.rem(q, half)
        sweep = jnp.minimum(phase, 1)
        source = sweep * (1 + half * (q // half)) + (1 - sweep) * zero_slot * ((q + last_q - 1) // last_q)
        sign = jnp.where((sweep == 0) & (q > 0), -1.0, 1.0).astype(jnp.float32)
        old, new, keep = jnp.float32(0.0), sign * jnp.float32(inv_centre), jnp.float32(0.0)
        for j, (wo, wn) in enumerate(weights):
            old = jnp.where(phase == j + 1, jnp.float32(wo), old)
            new = jnp.where(phase == j + 1, jnp.float32(wn), new)
            keep = jnp.where(phase == j + 1, jnp.float32(1.0), keep)
        v = v_ref.at[q]
        v_new = v_ref.at[q + 1]
        zero8 = jnp.zeros((8, X), jnp.float32)
        acc = {"u": zero8, "s": zero8, "v": zero8}

        def fold(name, value):
            for j in range(0, Y, 8):
                acc[name] = acc[name] + value[j:j + 8]

        def post_u(k, value):
            u_ref[Y + k * Y:2 * Y + k * Y, :] = value
            fold("u", value * value)

        def post_t(k, t):
            rows = slice(k * Y, (k + 1) * Y)
            vrows = slice(Y + k * Y, 2 * Y + k * Y)
            t = t * inv36
            src = e_ref[source, rows, :]
            defect = src - t
            e_ref[q + 1, rows, :] = sign * defect
            upd = old * d_ref[rows, :] + new * defect
            d_ref[rows, :] = upd
            was = v[vrows, :]
            z = keep * was + upd
            v_new[vrows, :] = z
            fold("s", src * z)
            fold("v", was * t)

        k_step(0, v, u_ref, Y, post_u)
        sums_u[...] = acc["u"]
        pl.when(q == last_q)(red_first)
        k_step(1, u_ref, t_ref, 0, post_t, lambda: pl.when(q == last_q)(red_second))
        sums_s[q] = acc["s"]
        sums_v[q] = acc["v"]
        return carry

    lax.fori_loop(0, last_q + 1, q_body, 0)

    red_start(2, red_finish(0))
    totals = jnp.sum(red_finish(2), axis=1, keepdims=True)
    e0, g1, g2 = totals[0:1], totals[1:2], totals[2:3]
    g3 = totals[3:4] * inv36
    alpha = e0 / g1
    e1 = e0 - 2.0 * alpha * g1 + alpha * alpha * g2
    keep = 1.0 + e1 / e0
    den = keep * keep * g1 - 2.0 * keep * alpha * g2 + alpha * alpha * g3
    alpha1 = e1 / den
    p = alpha + alpha1 * keep
    q = alpha1 * alpha
    for k in range(Z):
        rows = slice(k * Y, (k + 1) * Y)
        vrows = slice(Y + k * Y, 2 * Y + k * Y)
        x_ref[rows, :] = v_ref[0, vrows, :] + p * v_ref[half, vrows, :] - q * v_ref[last_q, vrows, :]
        r_ref[rows, :] = e_ref[1, rows, :] - p * e_ref[half + 1, rows, :] + q * e_ref[last_q + 1, rows, :]


def body(sizes, right_side, initial, kappa_sq):
    Z, Y, X = right_side.shape
    N = Z * Y
    f32 = jnp.float32
    flat = lambda a: a.reshape(N, X)
    vm = pl.BlockSpec(memory_space=pltpu.VMEM)
    hbm = pl.BlockSpec(memory_space=pltpu.HBM)
    big = max(sizes.values())
    count = 2 * SWEEPS + 1
    out = pl.pallas_call(
        functools.partial(kernel, sizes, (Z, Y, X)),
        out_shape=[jax.ShapeDtypeStruct((N, X), f32)] * 2,
        in_specs=[hbm] * 3,
        out_specs=[vm] * 2,
        scratch_shapes=[
            pltpu.VMEM((count + 1, N + 2 * Y, X), f32),
            pltpu.VMEM((count + 2, N, X), f32),
            pltpu.VMEM((N + 2 * Y, X), f32),
            pltpu.VMEM((N, X), f32),
            pltpu.VMEM((N, X), f32),
            pltpu.VMEM((N, X), f32),
            pltpu.VMEM((2, Y, X), f32),
            pltpu.VMEM((2, 2, Z, X), f32),
            pltpu.VMEM((2, 2, Y, X), f32),
            pltpu.VMEM((2, 2, Z, X), f32),
            pltpu.VMEM((2, 2, Y, X), f32),
            pltpu.VMEM((count, 8, X), f32),
            pltpu.VMEM((count, 8, X), f32),
            pltpu.VMEM((8, X), f32),
            pltpu.VMEM((3, 8, X), f32),
        ] + [pltpu.VMEM((sizes[a], 8, X), f32) for a in AXES] + [
            pltpu.SemaphoreType.DMA((2, 3, 2)),
            pltpu.SemaphoreType.DMA((2, 3, 2)),
            pltpu.SemaphoreType.DMA((3, big)),
            pltpu.SemaphoreType.DMA((3, big)),
            pltpu.SemaphoreType.DMA((3,)),
        ],
        compiler_params=pltpu.CompilerParams(
            collective_id=0, has_side_effects=True, vmem_limit_bytes=63 * 1024 * 1024),
        name="cg",
    )(flat(right_side), flat(initial), flat(kappa_sq))
    return tuple(o.reshape(Z, Y, X) for o in out)


def solution(mesh):
    spec = P("gz", "gy", "gx")
    sizes = {a: mesh.shape[a] for a in AXES}
    return jax.shard_map(functools.partial(body, sizes), mesh=mesh, in_specs=(spec,) * 3,
                         out_specs=(spec,) * 2, check_vma=False)
```

time: 59.2 us -> 59.1 us (level)
  local copies, waits for them, and re-layouts: 4.25 us -> 2.42 us
  Pallas kernels: 54.1 us -> 55.9 us
    unnamed x8 -> x4, local copies, waits for them, and re-layouts: 4.25 us -> 2.42 us
    pallas_call x1, Pallas kernels: 54.1 us -> 55.9 us  [body(): pl.pallas_call(functools.partial(kernel, sizes, (Z, Y, X)), out_shape=[ja...]
where the time goes in v2:
time: 59.1 us; the launch traced here: 58.9 us
  Pallas kernels  55.9 us (95%)
  local copies, waits for them, and re-layouts  2.42 us (4%)
  between operations  0.65 us (1%)
    pallas_call x1, Pallas kernels, body(): pl.pallas_call(functools.partial(kernel, sizes, (Z, Y, X)), out_shape=[ja...  55.9 us
    unnamed x4, local copies, waits for them, and re-layouts  2.42 us

profile of v2, /device:TPU:0, one launch (start us, length us, event | category | flops | bytes accessed | tf_op | source)
XLA Modules:
  0.0 58.9 jit_solution(17113892329148636800)
XLA Ops:
  0.6 55.9 %cg.1 = (f32[512,128]{1,0:T(8,128)}, f32[512,128]{1,0:T(8,128)}) custom-call(f32[512,128]{1,0:T(8,128)} %bitcast.5, f32[512,128]{1,0:T(8,128)} %bitcast.6, f32[512,128]{1,0:T(8,128)} %bitcast.7), custom_call_target="tpu_custom_call" | custom-call | tf_op jit(solution)/shard_map/cg/pallas_call | solution.py:267
  56.5 0.0 copy-start
  56.5 1.7 %copy.7 = f32[32,16,128]{2,1,0:T(8,128)} copy(f32[32,16,128]{2,1,0:T(8,128)} %bitcast.9) | data formatting | bytes 524288
  58.2 0.0 copy-done
  58.2 0.7 %copy.8 = f32[32,16,128]{2,1,0:T(8,128)} copy(f32[32,16,128]{2,1,0:T(8,128)S(1)} %bitcast.8) | data formatting | bytes 524288
Async XLA Ops:
  56.5 1.7 %copy-start = (f32[512,128]{1,0:T(8,128)S(1)}, f32[512,128]{1,0:T(8,128)}, u32[]{:S(2)}) copy-start(f32[512,128]{1,0:T(8,128)} %get-tuple-element.5) | copy-start | bytes 786436

commit v3 on v2

v3 whole, which is shorter than its diff:
```python
import functools
import jax
import jax.numpy as jnp
from jax import lax
from jax.experimental import pallas as pl
from jax.experimental.pallas import tpu as pltpu
from jax.sharding import PartitionSpec as P

SWEEPS = 3
cheb_high = 7.2
cheb_low = 0.072
MESH = pl.DeviceIdType.MESH
AXES = ("gx", "gy", "gz")
DIRECTIONS = [(z, y, x) for z in (-1, 0, 1) for y in (-1, 0, 1) for x in (-1, 0, 1)
              if 1 <= abs(z) + abs(y) + abs(x) <= 2]


def group_size(sizes, axes):
    size = 1
    for a in axes:
        size *= sizes[a]
    return size


def rank(sizes, where, axes):
    index = 0
    for a in axes:
        index = index * sizes[a] + where[a]
    return index


def peers(sizes, me, axes):
    found = []
    for k in range(1, group_size(sizes, axes)):
        to, origin, left = {}, {}, k
        for a in reversed(axes):
            shift, left = left % sizes[a], left // sizes[a]
            to[a] = lax.rem(me[a] + shift, sizes[a])
            origin[a] = lax.rem(me[a] + sizes[a] - shift, sizes[a])
        found.append((to, origin))
    return found


def sweep_weights():
    centre = (cheb_high + cheb_low) / 2.0
    half_width = (cheb_high - cheb_low) / 2.0
    sigma = centre / half_width
    old = 1.0 / sigma
    weights = []
    for _ in range(SWEEPS - 1):
        new = 1.0 / (2.0 * sigma - old)
        weights.append((new * old, 2.0 * new / half_width))
        old = new
    return 1.0 / centre, weights


def kernel(sizes, phases, shape, b_hbm, x0_hbm, kap_hbm, x_ref, r_ref,
           v_ref, e_ref, u_ref, t_ref, c_ref, d_ref,
           send, xhalo, yhalo, zhalo, zyhalo, zxhalo, yxhalo, cz_ref, cy_ref, cx_ref,
           sums_s, sums_v, sums_u, part, gather_a, gather_b, gather_c,
           send_sem, recv_sem, red_send, red_recv, in_sem):
    Z, Y, X = shape
    N = Z * Y
    me = {a: lax.axis_index(a) for a in AXES}
    inv_centre, weights = sweep_weights()
    inv36 = 1.0 / 36.0
    half = SWEEPS
    last_q = 2 * half
    zero_slot = last_q + 2

    loads = [pltpu.make_async_copy(kap_hbm, c_ref, in_sem.at[0]),
             pltpu.make_async_copy(x0_hbm, v_ref.at[0, pl.ds(Y, N)], in_sem.at[1]),
             pltpu.make_async_copy(b_hbm, e_ref.at[0], in_sem.at[2])]
    for load in loads:
        load.start()

    for halo in (xhalo, yhalo, zhalo, zyhalo, zxhalo, yxhalo):
        halo[...] = jnp.zeros_like(halo)

    def offset(d):
        return {a: me[a] + s for a, s in zip(("gz", "gy", "gx"), d) if s}

    def has(d):
        cond = None
        for a, s in zip(("gz", "gy", "gx"), d):
            if s:
                one = me[a] > 0 if s < 0 else me[a] < sizes[a] - 1
                cond = one if cond is None else cond & one
        return cond

    DIRS = [d for d in DIRECTIONS
            if all(s == 0 or sizes[a] > 1 for a, s in zip(("gz", "gy", "gx"), d))]

    barrier = pltpu.get_barrier_semaphore()
    count = 0
    for d in DIRS:
        cond = has(d)

        def greet(d=d):
            pl.semaphore_signal(barrier, inc=1, device_id=offset(d), device_id_type=MESH)
        pl.when(cond)(greet)
        count = count + jnp.where(cond, 1, 0)
    for axes in phases:
        for peer in peers(sizes, me, axes):
            pl.semaphore_signal(barrier, inc=1, device_id=peer[0], device_id_type=MESH)
            count = count + 1

    guard = jnp.zeros((Y, X), jnp.float32)
    for j in range(last_q + 2):
        v_ref[j, 0:Y, :] = guard
        v_ref[j, Y + N:2 * Y + N, :] = guard
    u_ref[0:Y, :] = guard
    u_ref[Y + N:2 * Y + N, :] = guard
    for k in range(Z):
        e_ref[zero_slot, k * Y:(k + 1) * Y, :] = guard
        d_ref[k * Y:(k + 1) * Y, :] = guard

    lane = lax.broadcasted_iota(jnp.int32, (Y, X), 1)
    row = lax.broadcasted_iota(jnp.int32, (Y, X), 0)
    quarter, place = lane // 4, lane % 4
    left_half = place < 2
    first_x, last_x = lane == 0, lane == X - 1
    edge_x = first_x | last_x
    first_y, last_y = row == 0, row == Y - 1
    lane_z = lax.broadcasted_iota(jnp.int32, (Z, X), 1)
    row_z = lax.broadcasted_iota(jnp.int32, (Z, X), 0)

    at_lo, at_x, at_hi = Z, 2 * Z, 2 * Z + Y

    def pack_y(slot, src, off):
        for at, y in ((0, 1), (at_lo, 0), (at_hi, Y - 1), (at_hi + Z, Y - 2)):
            send[slot, at:at + Z, :] = src[pl.ds(off + y, Z, stride=Y), :]

    def pack_x(slot, src, off):
        acc = jnp.zeros((Y, X), jnp.float32)
        for k in range(Z):
            v = src[off + k * Y:off + (k + 1) * Y, :]
            acc = jnp.where(quarter == k, pltpu.roll(v, (2 + 4 * k) % X, 1), acc)
        send[slot, at_x:at_x + Y, :] = acc

    def source_of(d, slot, src, off):
        dz, dy, dx = d
        out = send.at[slot]
        if dx:
            if dy == 0:
                return out.at[pl.ds(at_x, Y)]
            return out.at[pl.ds(at_lo if dy < 0 else at_x, Z + Y)]
        if dy and dz:
            return out.at[pl.ds((at_lo if dy < 0 else at_hi) + (0 if dz < 0 else Z - 8), 8)]
        if dy:
            return out.at[pl.ds(0 if dy < 0 else at_hi, 2 * Z)]
        return src.at[pl.ds(off if dz < 0 else off + N - 2 * Y, 2 * Y)]

    def halo_of(d, slot):
        sz, sy, sx = (0 if s > 0 else 1 for s in d)
        dz, dy, dx = d
        if dx and dy:
            return yxhalo.at[slot, sy, sx]
        if dx and dz:
            return zxhalo.at[slot, sz, sx]
        if dx:
            return xhalo.at[slot, sx]
        if dy and dz:
            return zyhalo.at[slot, sz, sy]
        return yhalo.at[slot, sy] if dy else zhalo.at[slot, sz]

    def copy_to(d, slot, src, off):
        i = DIRECTIONS.index(d)
        return pltpu.make_async_remote_copy(
            src_ref=source_of(d, slot, src, off), dst_ref=halo_of(d, slot),
            send_sem=send_sem.at[slot, i], recv_sem=recv_sem.at[slot, i],
            device_id=offset(d), device_id_type=MESH)

    def copy_from(d, slot, src, off):
        back = tuple(-s for s in d)
        i = DIRECTIONS.index(back)
        return pltpu.make_async_remote_copy(
            src_ref=source_of(back, slot, src, off), dst_ref=halo_of(back, slot),
            send_sem=send_sem.at[slot, i], recv_sem=recv_sem.at[slot, i],
            device_id=offset(d), device_id_type=MESH)

    def start_all(slot, src, off):
        def go(want):
            for d in DIRS:
                if want(d):
                    pl.when(has(d))(lambda d=d: copy_to(d, slot, src, off).start())

        go(lambda d: d[1] == 0 and d[2] == 0)
        pack_x(slot, src, off)
        pack_y(slot, src, off)
        go(lambda d: d[2] != 0)
        go(lambda d: d[1] != 0 and d[2] == 0)

    def finish_all(slot, src, off):
        for d in DIRS:
            def done(d=d):
                copy_from(d, slot, src, off).wait_recv()
                copy_to(d, slot, src, off).wait_send()
            pl.when(has(d))(done)

    def faces(slot):
        z1 = [zhalo[slot, 0, Y:2 * Y, :], zhalo[slot, 1, 0:Y, :]]
        y1 = [yhalo[slot, 0, 0:Z, :], yhalo[slot, 1, Z:2 * Z, :]]
        x1 = jnp.where(left_half, xhalo[slot, 0], xhalo[slot, 1])
        return z1, y1, x1

    def pairs_of(columns):
        return jnp.where(place == 2, pltpu.roll(columns, 1, 1), pltpu.roll(columns, X - 1, 1))

    def edge_of(pairs, k):
        return jnp.where(edge_x, pltpu.roll(pairs, (2 * X - 2 - 4 * k) % X, 1), 0.0)

    def along_x(v, lanes):
        return (jnp.where(lanes == 0, 0.0, pltpu.roll(v, 1, 1))
                + jnp.where(lanes == X - 1, 0.0, pltpu.roll(v, X - 1, 1)))

    exists = {a: [jnp.where(me[a] > 0, 1.0, 0.0).astype(jnp.float32),
                  jnp.where(me[a] < sizes[a] - 1, 1.0, 0.0).astype(jnp.float32)] for a in AXES}

    def outer(slot, v, off):
        z1, y1, x1 = faces(slot)
        z2 = [zhalo[slot, 0, 0:Y, :], zhalo[slot, 1, Y:2 * Y, :]]
        y2 = [yhalo[slot, 0, Z:2 * Z, :], yhalo[slot, 1, 0:Z, :]]
        zx = [jnp.where(left_half, zxhalo[slot, s, 0], zxhalo[slot, s, 1]) for s in (0, 1)]
        yx = [jnp.where(left_half, yxhalo[slot, s, 0, r:r + Y, :], yxhalo[slot, s, 1, r:r + Y, :])
              for s, r in ((0, 0), (1, Z))]
        zy = [[zyhalo[slot, sz, sy, r:r + 1, :] for sy in (0, 1)] for sz, r in ((0, 7), (1, 0))]
        uz, uy = [], []
        for s, k in ((0, 0), (1, Z - 1)):
            f = z1[s]
            total = z2[s] + v[off + k * Y:off + (k + 1) * Y, :] + along_x(f, lane)
            total = total + edge_of(pairs_of(zx[s]), Z - 1 - k)
            total = total + jnp.where(first_y, zy[s][0], pltpu.roll(f, 1, 0))
            total = total + jnp.where(last_y, zy[s][1], pltpu.roll(f, Y - 1, 0))
            uz.append((cz_ref[s] * f - total) * exists["gz"][s])
        for s, at, r in ((0, at_lo, Y), (1, at_hi, 0)):
            f = y1[s]
            total = y2[s] + send[slot, at:at + Z, :]
            total = total + jnp.where(lane_z == 0, pltpu.roll(yxhalo[slot, s, 0, r:r + Z, :], 1, 1),
                                      pltpu.roll(f, 1, 1))
            total = total + jnp.where(lane_z == X - 1,
                                      pltpu.roll(yxhalo[slot, s, 1, r:r + Z, :], X - 1, 1),
                                      pltpu.roll(f, X - 1, 1))
            total = total + jnp.where(row_z == 0, zy[0][s], pltpu.roll(f, 1, 0))
            total = total + jnp.where(row_z == Z - 1, zy[1][s], pltpu.roll(f, Z - 1, 0))
            uy.append((cy_ref[s] * f - total) * exists["gy"][s])
        own = send[slot, at_x:at_x + Y, :]
        total = jnp.where(place == 1, pltpu.roll(x1, 1, 1) + pltpu.roll(own, X - 1, 1),
                          pltpu.roll(x1, X - 1, 1) + pltpu.roll(own, 1, 1))
        total = total + jnp.where(first_y, yx[0][Y - 1:Y, :], pltpu.roll(x1, 1, 0))
        total = total + jnp.where(last_y, yx[1][0:1, :], pltpu.roll(x1, Y - 1, 0))
        total = total + jnp.where(lane < 4, pltpu.roll(zx[0], 4, 1), pltpu.roll(x1, 4, 1))
        total = total + jnp.where(lane >= X - 4, pltpu.roll(zx[1], X - 4, 1),
                                  pltpu.roll(x1, X - 4, 1))
        ux = (cx_ref[...] * x1 - total) * jnp.where(left_half, exists["gx"][0], exists["gx"][1])
        return uz, uy, ux

    def k_inner(src, dst, dst_off):
        for k in range(Z):
            i = Y + k * Y
            v = src[i:i + Y, :]
            total = src[i - Y:i, :] + src[i + Y:i + 2 * Y, :] + along_x(v, lane)
            total = total + jnp.where(first_y, 0.0, src[i - 1:i - 1 + Y, :])
            total = total + jnp.where(last_y, 0.0, src[i + 1:i + 1 + Y, :])
            dst[dst_off + k * Y:dst_off + (k + 1) * Y, :] = c_ref[k * Y:(k + 1) * Y, :] * v - total

    def k_fix(dst, dst_off, halo, post):
        hz, hy, hx = halo
        for s, first in ((0, 0), (1, N - Y)):
            rows = slice(dst_off + first, dst_off + first + Y)
            dst[rows, :] = dst[rows, :] - hz[s]
        for s, first in ((0, 0), (1, Y - 1)):
            rows = pl.ds(dst_off + first, Z, stride=Y)
            dst[rows, :] = dst[rows, :] - hy[s]
        pairs = pairs_of(hx)
        for k in range(Z):
            rows = slice(dst_off + k * Y, dst_off + (k + 1) * Y)
            post(k, dst[rows, :] - edge_of(pairs, k))

    loads[0].wait()
    pl.semaphore_wait(barrier, count)
    start_all(2, c_ref, 0)
    loads[1].wait()
    start_all(0, v_ref.at[0], Y)
    loads[2].wait()
    finish_all(2, c_ref, 0)
    kz, ky, kx = faces(2)
    for s in (0, 1):
        cz_ref[s] = 6.0 + kz[s]
        cy_ref[s] = 6.0 + ky[s]
    cx_ref[...] = 6.0 + kx
    for k in range(Z):
        rows = slice(k * Y, (k + 1) * Y)
        c_ref[rows, :] = 6.0 + c_ref[rows, :]

    gathers = (gather_a, gather_b, gather_c)

    def red_start(i, value):
        part[i] = value
        gathers[i][pl.ds(rank(sizes, me, phases[i]), 1)] = value[None]
        for k, (peer, _) in enumerate(peers(sizes, me, phases[i])):
            pltpu.make_async_remote_copy(
                src_ref=part.at[i], dst_ref=gathers[i].at[rank(sizes, me, phases[i])],
                send_sem=red_send.at[i, k], recv_sem=red_recv.at[i, k],
                device_id=peer, device_id_type=MESH).start()

    def red_finish(i):
        for k, (peer, origin) in enumerate(peers(sizes, me, phases[i])):
            copy = pltpu.make_async_remote_copy(
                src_ref=part.at[i], dst_ref=gathers[i].at[rank(sizes, origin, phases[i])],
                send_sem=red_send.at[i, k], recv_sem=red_recv.at[i, k],
                device_id=peer, device_id_type=MESH)
            copy.wait_recv()
            copy.wait_send()
        total = gathers[i][0]
        for j in range(1, group_size(sizes, phases[i])):
            total = total + gathers[i][j]
        return total

    def red_first():
        rows8 = lax.broadcasted_iota(jnp.int32, (8, X), 0)
        mine = jnp.zeros((8, X), jnp.float32)
        for j, value in enumerate((sums_s[half - 1], sums_v[half], sums_s[last_q - 1], sums_u[...])):
            mine = jnp.where(rows8 == j, jnp.sum(value, axis=0, keepdims=True), mine)
        red_start(0, mine)

    def q_body(q, carry):
        phase = lax.rem(q, half)
        sweep = jnp.minimum(phase, 1)
        source = sweep * (1 + half * (q // half)) + (1 - sweep) * zero_slot * ((q + last_q - 1) // last_q)
        sign = jnp.where((sweep == 0) & (q > 0), -1.0, 1.0).astype(jnp.float32)
        old, new, keep = jnp.float32(0.0), sign * jnp.float32(inv_centre), jnp.float32(0.0)
        for j, (wo, wn) in enumerate(weights):
            old = jnp.where(phase == j + 1, jnp.float32(wo), old)
            new = jnp.where(phase == j + 1, jnp.float32(wn), new)
            keep = jnp.where(phase == j + 1, jnp.float32(1.0), keep)
        v = v_ref.at[q]
        v_new = v_ref.at[q + 1]
        zero8 = jnp.zeros((8, X), jnp.float32)
        acc = {"u": zero8, "s": zero8, "v": zero8}

        def fold(name, value):
            for j in range(0, Y, 8):
                acc[name] = acc[name] + value[j:j + 8]

        def post_u(k, value):
            u_ref[Y + k * Y:2 * Y + k * Y, :] = value
            fold("u", value * value)

        def post_t(k, t):
            rows = slice(k * Y, (k + 1) * Y)
            vrows = slice(Y + k * Y, 2 * Y + k * Y)
            t = t * inv36
            src = e_ref[source, rows, :]
            defect = src - t
            e_ref[q + 1, rows, :] = sign * defect
            upd = old * d_ref[rows, :] + new * defect
            d_ref[rows, :] = upd
            was = v[vrows, :]
            z = keep * was + upd
            v_new[vrows, :] = z
            fold("s", src * z)
            fold("v", was * t)

        slot = lax.rem(q, 2)
        pl.when(q > 0)(lambda: start_all(slot, v, Y))
        k_inner(v, u_ref, Y)
        finish_all(slot, v, Y)
        k_fix(u_ref, Y, faces(slot), post_u)
        sums_u[...] = acc["u"]
        pl.when(q == last_q)(red_first)
        k_inner(u_ref, t_ref, 0)
        k_fix(t_ref, 0, outer(slot, v, Y), post_t)
        sums_s[q] = acc["s"]
        sums_v[q] = acc["v"]
        return carry

    lax.fori_loop(0, last_q + 1, q_body, 0)

    total = red_finish(0)
    for i in range(1, len(phases)):
        red_start(i, total)
        total = red_finish(i)
    totals = jnp.sum(total, axis=1, keepdims=True)
    e0, g1, g2 = totals[0:1], totals[1:2], totals[2:3]
    g3 = totals[3:4] * inv36
    alpha = e0 / g1
    e1 = e0 - 2.0 * alpha * g1 + alpha * alpha * g2
    keep = 1.0 + e1 / e0
    den = keep * keep * g1 - 2.0 * keep * alpha * g2 + alpha * alpha * g3
    alpha1 = e1 / den
    p = alpha + alpha1 * keep
    q = alpha1 * alpha
    for k in range(Z):
        rows = slice(k * Y, (k + 1) * Y)
        vrows = slice(Y + k * Y, 2 * Y + k * Y)
        x_ref[rows, :] = v_ref[0, vrows, :] + p * v_ref[half, vrows, :] - q * v_ref[last_q, vrows, :]
        r_ref[rows, :] = e_ref[1, rows, :] - p * e_ref[half + 1, rows, :] + q * e_ref[last_q + 1, rows, :]


def body(sizes, right_side, initial, kappa_sq):
    Z, Y, X = right_side.shape
    N = Z * Y
    f32 = jnp.float32
    flat = lambda a: a.reshape(N, X)
    vm = pl.BlockSpec(memory_space=pltpu.VMEM)
    hbm = pl.BlockSpec(memory_space=pltpu.HBM)
    assert 4 * Z == X and Y % 8 == 0
    phases = [("gx", "gy"), ("gz",)] if sizes["gx"] * sizes["gy"] <= 16 else [(a,) for a in AXES]
    groups = [group_size(sizes, axes) for axes in phases] + [1]
    slots = 3
    count = 2 * SWEEPS + 1
    out = pl.pallas_call(
        functools.partial(kernel, sizes, phases, (Z, Y, X)),
        out_shape=[jax.ShapeDtypeStruct((N, X), f32)] * 2,
        in_specs=[hbm] * 3,
        out_specs=[vm] * 2,
        scratch_shapes=[
            pltpu.VMEM((count + 1, N + 2 * Y, X), f32),
            pltpu.VMEM((count + 2, N, X), f32),
            pltpu.VMEM((N + 2 * Y, X), f32),
            pltpu.VMEM((N, X), f32),
            pltpu.VMEM((N, X), f32),
            pltpu.VMEM((N, X), f32),
            pltpu.VMEM((slots, 4 * Z + Y, X), f32),
            pltpu.VMEM((slots, 2, Y, X), f32),
            pltpu.VMEM((slots, 2, 2 * Z, X), f32),
            pltpu.VMEM((slots, 2, 2 * Y, X), f32),
            pltpu.VMEM((slots, 2, 2, 8, X), f32),
            pltpu.VMEM((slots, 2, 2, Y, X), f32),
            pltpu.VMEM((slots, 2, 2, Z + Y, X), f32),
            pltpu.VMEM((2, Y, X), f32),
            pltpu.VMEM((2, Z, X), f32),
            pltpu.VMEM((Y, X), f32),
            pltpu.VMEM((count, 8, X), f32),
            pltpu.VMEM((count, 8, X), f32),
            pltpu.VMEM((8, X), f32),
            pltpu.VMEM((3, 8, X), f32),
        ] + [pltpu.VMEM(((groups + [1])[i], 8, X), f32) for i in range(3)] + [
            pltpu.SemaphoreType.DMA((slots, len(DIRECTIONS))),
            pltpu.SemaphoreType.DMA((slots, len(DIRECTIONS))),
            pltpu.SemaphoreType.DMA((3, max(groups))),
            pltpu.SemaphoreType.DMA((3, max(groups))),
            pltpu.SemaphoreType.DMA((3,)),
        ],
        compiler_params=pltpu.CompilerParams(
            collective_id=0, has_side_effects=True, vmem_limit_bytes=63 * 1024 * 1024),
        name="cg",
    )(flat(right_side), flat(initial), flat(kappa_sq))
    return tuple(o.reshape(Z, Y, X) for o in out)


def solution(mesh):
    spec = P("gz", "gy", "gx")
    sizes = {a: mesh.shape[a] for a in AXES}
    return jax.shard_map(functools.partial(body, sizes), mesh=mesh, in_specs=(spec,) * 3,
                         out_specs=(spec,) * 2, check_vma=False)
```

time: 59.1 us -> 46.7 us (0.79)
  Pallas kernels: 55.9 us -> 43.5 us
    pallas_call x1, Pallas kernels: 55.9 us -> 43.5 us  [body(): pl.pallas_call(functools.partial(kernel, sizes, phases, (Z, Y, X)), out_s...]
where the time goes in v3:
time: 46.7 us; the launch traced here: 46.5 us
  Pallas kernels  43.5 us (93%)
  local copies, waits for them, and re-layouts  2.42 us (5%)
  between operations  0.65 us (1%)
    pallas_call x1, Pallas kernels, body(): pl.pallas_call(functools.partial(kernel, sizes, phases, (Z, Y, X)), out_s...  43.5 us
    unnamed x4, local copies, waits for them, and re-layouts  2.42 us

profile of v3, /device:TPU:0, one launch (start us, length us, event | category | flops | bytes accessed | tf_op | source)
XLA Modules:
  0.0 46.5 jit_solution(7323543914557526156)
XLA Ops:
  0.6 43.5 %cg.1 = (f32[512,128]{1,0:T(8,128)}, f32[512,128]{1,0:T(8,128)}) custom-call(f32[512,128]{1,0:T(8,128)} %bitcast.5, f32[512,128]{1,0:T(8,128)} %bitcast.6, f32[512,128]{1,0:T(8,128)} %bitcast.7), custom_call_target="tpu_custom_call" | custom-call | tf_op jit(solution)/shard_map/cg/pallas_call | solution.py:413
  44.1 0.0 copy-start
  44.1 1.7 %copy.7 = f32[32,16,128]{2,1,0:T(8,128)} copy(f32[32,16,128]{2,1,0:T(8,128)} %bitcast.9) | data formatting | bytes 524288
  45.8 0.0 copy-done
  45.8 0.7 %copy.8 = f32[32,16,128]{2,1,0:T(8,128)} copy(f32[32,16,128]{2,1,0:T(8,128)S(1)} %bitcast.8) | data formatting | bytes 524288
Async XLA Ops:
  44.1 1.7 %copy-start = (f32[512,128]{1,0:T(8,128)S(1)}, f32[512,128]{1,0:T(8,128)}, u32[]{:S(2)}) copy-start(f32[512,128]{1,0:T(8,128)} %get-tuple-element.5) | copy-start | bytes 786436

commit v4 on v3

--- a/solution.py
+++ b/solution.py
@@ -55,7 +55,7 @@
 
 
 def kernel(sizes, phases, shape, b_hbm, x0_hbm, kap_hbm, x_ref, r_ref,
-           v_ref, e_ref, u_ref, t_ref, c_ref, d_ref,
+           v_ref, e_ref, u_ref, hrow, c_ref, d_ref,
            send, xhalo, yhalo, zhalo, zyhalo, zxhalo, yxhalo, cz_ref, cy_ref, cx_ref,
            sums_s, sums_v, sums_u, part, gather_a, gather_b, gather_c,
            send_sem, recv_sem, red_send, red_recv, in_sem):
@@ -77,19 +77,34 @@
     for halo in (xhalo, yhalo, zhalo, zyhalo, zxhalo, yxhalo):
         halo[...] = jnp.zeros_like(halo)
 
+    other_x = sizes["gx"] == 2
+
     def offset(d):
-        return {a: me[a] + s for a, s in zip(("gz", "gy", "gx"), d) if s}
+        to = {a: me[a] + s for a, s in zip(("gz", "gy", "gx"), d) if s}
+        if other_x and d[2]:
+            to["gx"] = 1 - me["gx"]
+        return to
 
     def has(d):
         cond = None
         for a, s in zip(("gz", "gy", "gx"), d):
-            if s:
+            if s and not (other_x and a == "gx"):
                 one = me[a] > 0 if s < 0 else me[a] < sizes[a] - 1
                 cond = one if cond is None else cond & one
         return cond
 
+    def when(cond, fn):
+        if cond is None:
+            fn()
+        else:
+            pl.when(cond)(fn)
+
     DIRS = [d for d in DIRECTIONS
-            if all(s == 0 or sizes[a] > 1 for a, s in zip(("gz", "gy", "gx"), d))]
+            if all(s == 0 or sizes[a] > 1 for a, s in zip(("gz", "gy", "gx"), d))
+            and not (other_x and d[2] < 0)]
+
+    def reverse(d):
+        return (-d[0], -d[1], d[2] if other_x else -d[2])
 
     barrier = pltpu.get_barrier_semaphore()
     count = 0
@@ -98,8 +113,8 @@
 
         def greet(d=d):
             pl.semaphore_signal(barrier, inc=1, device_id=offset(d), device_id_type=MESH)
-        pl.when(cond)(greet)
-        count = count + jnp.where(cond, 1, 0)
+        when(cond, greet)
+        count = count + (1 if cond is None else jnp.where(cond, 1, 0))
     for axes in phases:
         for peer in peers(sizes, me, axes):
             pl.semaphore_signal(barrier, inc=1, device_id=peer[0], device_id_type=MESH)
@@ -151,8 +166,9 @@
             return out.at[pl.ds(0 if dy < 0 else at_hi, 2 * Z)]
         return src.at[pl.ds(off if dz < 0 else off + N - 2 * Y, 2 * Y)]
 
-    def halo_of(d, slot):
-        sz, sy, sx = (0 if s > 0 else 1 for s in d)
+    def halo_of(d, slot, side_x):
+        sz, sy = (0 if s > 0 else 1 for s in d[:2])
+        sx = side_x if other_x else (0 if d[2] > 0 else 1)
         dz, dy, dx = d
         if dx and dy:
             return yxhalo.at[slot, sy, sx]
@@ -167,36 +183,45 @@
     def copy_to(d, slot, src, off):
         i = DIRECTIONS.index(d)
         return pltpu.make_async_remote_copy(
-            src_ref=source_of(d, slot, src, off), dst_ref=halo_of(d, slot),
+            src_ref=source_of(d, slot, src, off), dst_ref=halo_of(d, slot, me["gx"]),
             send_sem=send_sem.at[slot, i], recv_sem=recv_sem.at[slot, i],
             device_id=offset(d), device_id_type=MESH)
 
     def copy_from(d, slot, src, off):
-        back = tuple(-s for s in d)
+        back = reverse(d)
         i = DIRECTIONS.index(back)
         return pltpu.make_async_remote_copy(
-            src_ref=source_of(back, slot, src, off), dst_ref=halo_of(back, slot),
+            src_ref=source_of(back, slot, src, off), dst_ref=halo_of(back, slot, 1 - me["gx"]),
             send_sem=send_sem.at[slot, i], recv_sem=recv_sem.at[slot, i],
             device_id=offset(d), device_id_type=MESH)
 
-    def start_all(slot, src, off):
+    def start_all(slot, src, off, packed_x=False):
         def go(want):
             for d in DIRS:
                 if want(d):
-                    pl.when(has(d))(lambda d=d: copy_to(d, slot, src, off).start())
-
-        go(lambda d: d[1] == 0 and d[2] == 0)
-        pack_x(slot, src, off)
+                    when(has(d), lambda d=d: copy_to(d, slot, src, off).start())
+
+        if packed_x:
+            go(lambda d: d[2] != 0 and d[1] == 0)
         pack_y(slot, src, off)
-        go(lambda d: d[2] != 0)
-        go(lambda d: d[1] != 0 and d[2] == 0)
-
-    def finish_all(slot, src, off):
+        if packed_x:
+            go(lambda d: d[2] != 0 and d[1] != 0)
+        go(lambda d: d[0] != 0 and d[1] != 0 and d[2] == 0)
+        go(lambda d: d[1] != 0 and d[0] == 0 and d[2] == 0)
+        go(lambda d: d[0] != 0 and d[1] == 0 and d[2] == 0)
+        if not packed_x:
+            pack_x(slot, src, off)
+            go(lambda d: d[2] != 0)
+
+    def finish(edges, slot, src, off):
         for d in DIRS:
+            if (sum(1 for s in d if s) > 1) != edges:
+                continue
+
             def done(d=d):
                 copy_from(d, slot, src, off).wait_recv()
                 copy_to(d, slot, src, off).wait_send()
-            pl.when(has(d))(done)
+            when(has(d), done)
 
     def faces(slot):
         z1 = [zhalo[slot, 0, Y:2 * Y, :], zhalo[slot, 1, 0:Y, :]]
@@ -264,18 +289,38 @@
             total = total + jnp.where(last_y, 0.0, src[i + 1:i + 1 + Y, :])
             dst[dst_off + k * Y:dst_off + (k + 1) * Y, :] = c_ref[k * Y:(k + 1) * Y, :] * v - total
 
-    def k_fix(dst, dst_off, halo, post):
+    def k_first(halo, post):
         hz, hy, hx = halo
-        for s, first in ((0, 0), (1, N - Y)):
-            rows = slice(dst_off + first, dst_off + first + Y)
-            dst[rows, :] = dst[rows, :] - hz[s]
-        for s, first in ((0, 0), (1, Y - 1)):
-            rows = pl.ds(dst_off + first, Z, stride=Y)
-            dst[rows, :] = dst[rows, :] - hy[s]
+        for s in (0, 1):
+            hrow[s] = hy[s]
         pairs = pairs_of(hx)
         for k in range(Z):
-            rows = slice(dst_off + k * Y, dst_off + (k + 1) * Y)
-            post(k, dst[rows, :] - edge_of(pairs, k))
+            total = edge_of(pairs, k)
+            total = total + jnp.where(first_y, hrow[0, k:k + 1, :], 0.0)
+            total = total + jnp.where(last_y, hrow[1, k:k + 1, :], 0.0)
+            if k == 0:
+                total = total + hz[0]
+            if k == Z - 1:
+                total = total + hz[1]
+            post(k, u_ref[Y + k * Y:2 * Y + k * Y, :] - total)
+
+    def k_second(halo, post):
+        hz, hy, hx = halo
+        u_ref[0:Y, :] = hz[0]
+        u_ref[Y + N:2 * Y + N, :] = hz[1]
+        for s in (0, 1):
+            hrow[s] = hy[s]
+        pairs = pairs_of(hx)
+        for k in range(Z):
+            i = Y + k * Y
+            f = u_ref[i:i + Y, :]
+            ends = pltpu.roll(pairs, (2 * X - 2 - 4 * k) % X, 1)
+            total = u_ref[i - Y:i, :] + u_ref[i + Y:i + 2 * Y, :]
+            total = total + jnp.where(first_x, ends, pltpu.roll(f, 1, 1))
+            total = total + jnp.where(last_x, ends, pltpu.roll(f, X - 1, 1))
+            total = total + jnp.where(first_y, hrow[0, k:k + 1, :], u_ref[i - 1:i - 1 + Y, :])
+            total = total + jnp.where(last_y, hrow[1, k:k + 1, :], u_ref[i + 1:i + 1 + Y, :])
+            post(k, c_ref[k * Y:(k + 1) * Y, :] * f - total)
 
     loads[0].wait()
     pl.semaphore_wait(barrier, count)
@@ -283,7 +328,8 @@
     loads[1].wait()
     start_all(0, v_ref.at[0], Y)
     loads[2].wait()
-    finish_all(2, c_ref, 0)
+    finish(False, 2, c_ref, 0)
+    finish(True, 2, c_ref, 0)
     kz, ky, kx = faces(2)
     for s in (0, 1):
         cz_ref[s] = 6.0 + kz[s]
@@ -337,7 +383,7 @@
         v = v_ref.at[q]
         v_new = v_ref.at[q + 1]
         zero8 = jnp.zeros((8, X), jnp.float32)
-        acc = {"u": zero8, "s": zero8, "v": zero8}
+        acc = {"u": zero8, "s": zero8, "v": zero8, "x": jnp.zeros((Y, X), jnp.float32)}
 
         def fold(name, value):
             for j in range(0, Y, 8):
@@ -361,16 +407,18 @@
             v_new[vrows, :] = z
             fold("s", src * z)
             fold("v", was * t)
+            acc["x"] = jnp.where(quarter == k, pltpu.roll(z, (2 + 4 * k) % X, 1), acc["x"])
 
         slot = lax.rem(q, 2)
-        pl.when(q > 0)(lambda: start_all(slot, v, Y))
         k_inner(v, u_ref, Y)
-        finish_all(slot, v, Y)
-        k_fix(u_ref, Y, faces(slot), post_u)
+        finish(False, slot, v, Y)
+        k_first(faces(slot), post_u)
         sums_u[...] = acc["u"]
         pl.when(q == last_q)(red_first)
-        k_inner(u_ref, t_ref, 0)
-        k_fix(t_ref, 0, outer(slot, v, Y), post_t)
+        finish(True, slot, v, Y)
+        k_second(outer(slot, v, Y), post_t)
+        send[1 - slot, at_x:at_x + Y, :] = acc["x"]
+        pl.when(q < last_q)(lambda: start_all(1 - slot, v_new, Y, packed_x=True))
         sums_s[q] = acc["s"]
         sums_v[q] = acc["v"]
         return carry
@@ -396,6 +444,22 @@
         vrows = slice(Y + k * Y, 2 * Y + k * Y)
         x_ref[rows, :] = v_ref[0, vrows, :] + p * v_ref[half, vrows, :] - q * v_ref[last_q, vrows, :]
         r_ref[rows, :] = e_ref[1, rows, :] - p * e_ref[half + 1, rows, :] + q * e_ref[last_q + 1, rows, :]
+
+
+PIECES = 4
+
+
+def hand_on(x_in, r_in, x_out, r_out, sem):
+    copies = []
+    for i, (src, dst) in enumerate(((x_in, x_out), (r_in, r_out))):
+        n = src.shape[0] // PIECES
+        for j in range(PIECES):
+            rows = pl.ds(j * n, n)
+            copies.append(pltpu.make_async_copy(src.at[rows], dst.at[rows], sem.at[i, j]))
+    for copy in copies:
+        copy.start()
+    for copy in copies:
+        copy.wait()
 
 
 def body(sizes, right_side, initial, kappa_sq):
@@ -419,7 +483,7 @@
             pltpu.VMEM((count + 1, N + 2 * Y, X), f32),
             pltpu.VMEM((count + 2, N, X), f32),
             pltpu.VMEM((N + 2 * Y, X), f32),
-            pltpu.VMEM((N, X), f32),
+            pltpu.VMEM((2, Z, X), f32),
             pltpu.VMEM((N, X), f32),
             pltpu.VMEM((N, X), f32),
             pltpu.VMEM((slots, 4 * Z + Y, X), f32),
@@ -447,6 +511,15 @@
             collective_id=0, has_side_effects=True, vmem_limit_bytes=63 * 1024 * 1024),
         name="cg",
     )(flat(right_side), flat(initial), flat(kappa_sq))
+    out = pl.pallas_call(
+        hand_on,
+        out_shape=[jax.ShapeDtypeStruct((N, X), f32)] * 2,
+        in_specs=[hbm] * 2,
+        out_specs=[hbm] * 2,
+        scratch_shapes=[pltpu.SemaphoreType.DMA((2, PIECES))],
+        compiler_params=pltpu.CompilerParams(vmem_limit_bytes=63 * 1024 * 1024),
+        name="hand_on",
+    )(*out)
     return tuple(o.reshape(Z, Y, X) for o in out)
 
 

time: 46.7 us -> 59.7 us (1.28)
  Pallas kernels: 43.5 us -> 58.9 us
  local copies, waits for them, and re-layouts: 2.42 us -> 0 us
    pallas_call x0 -> x1, Pallas kernels: none -> 17.1 us  [body(): pl.pallas_call(hand_on, out_shape=[jax.ShapeDtypeStruct((N, X), f32)] * 2...]
    unnamed x4 -> x0, local copies, waits for them, and re-layouts: 2.42 us -> none
    pallas_call x1, Pallas kernels: 43.5 us -> 41.8 us  [body(): pl.pallas_call(functools.partial(kernel, sizes, phases, (Z, Y, X)), out_s...]
where the time goes in v4:
time: 59.7 us; the launch traced here: 59.5 us
  Pallas kernels  58.9 us (99%)
  between operations  0.64 us (1%)
    pallas_call x1, Pallas kernels, body(): pl.pallas_call(functools.partial(kernel, sizes, phases, (Z, Y, X)), out_s...  41.8 us
    pallas_call x1, Pallas kernels, body(): pl.pallas_call(hand_on, out_shape=[jax.ShapeDtypeStruct((N, X), f32)] * 2...  17.1 us

profile of v4, /device:TPU:0, one launch (start us, length us, event | category | flops | bytes accessed | tf_op | source)
XLA Modules:
  0.0 59.5 jit_solution(12442925283045174356)
XLA Ops:
  0.6 41.8 %cg.1 = (f32[512,128]{1,0:T(8,128)}, f32[512,128]{1,0:T(8,128)}) custom-call(f32[512,128]{1,0:T(8,128)} %bitcast.5, f32[512,128]{1,0:T(8,128)} %bitcast.6, f32[512,128]{1,0:T(8,128)} %bitcast.7), custom_call_target="tpu_custom_call" | custom-call | tf_op jit(solution)/shard_map/cg/pallas_call | solution.py:477
  42.5 17.1 %hand_on.1 = (f32[512,128]{1,0:T(8,128)}, f32[512,128]{1,0:T(8,128)}) custom-call(f32[512,128]{1,0:T(8,128)} %get-tuple-element.6.x_in, f32[512,128]{1,0:T(8,128)} %get-tuple-element.7.r_in), custom_call_target="tpu_custom_call" | custom-call | tf_op jit(solution)/shard_map/hand_on/pallas_call | solution.py:514

commit v5 on v4

--- a/solution.py
+++ b/solution.py
@@ -55,7 +55,7 @@
 
 
 def kernel(sizes, phases, shape, b_hbm, x0_hbm, kap_hbm, x_ref, r_ref,
-           v_ref, e_ref, u_ref, hrow, c_ref, d_ref,
+           v, src_ref, v_hist, s_hist, u_ref, hrow, c_ref, d_ref,
            send, xhalo, yhalo, zhalo, zyhalo, zxhalo, yxhalo, cz_ref, cy_ref, cx_ref,
            sums_s, sums_v, sums_u, part, gather_a, gather_b, gather_c,
            send_sem, recv_sem, red_send, red_recv, in_sem):
@@ -66,11 +66,10 @@
     inv36 = 1.0 / 36.0
     half = SWEEPS
     last_q = 2 * half
-    zero_slot = last_q + 2
 
     loads = [pltpu.make_async_copy(kap_hbm, c_ref, in_sem.at[0]),
-             pltpu.make_async_copy(x0_hbm, v_ref.at[0, pl.ds(Y, N)], in_sem.at[1]),
-             pltpu.make_async_copy(b_hbm, e_ref.at[0], in_sem.at[2])]
+             pltpu.make_async_copy(x0_hbm, v.at[pl.ds(Y, N)], in_sem.at[1]),
+             pltpu.make_async_copy(b_hbm, src_ref, in_sem.at[2])]
     for load in loads:
         load.start()
 
@@ -121,13 +120,10 @@
             count = count + 1
 
     guard = jnp.zeros((Y, X), jnp.float32)
-    for j in range(last_q + 2):
-        v_ref[j, 0:Y, :] = guard
-        v_ref[j, Y + N:2 * Y + N, :] = guard
-    u_ref[0:Y, :] = guard
-    u_ref[Y + N:2 * Y + N, :] = guard
+    for ref in (v, u_ref):
+        ref[0:Y, :] = guard
+        ref[Y + N:2 * Y + N, :] = guard
     for k in range(Z):
-        e_ref[zero_slot, k * Y:(k + 1) * Y, :] = guard
         d_ref[k * Y:(k + 1) * Y, :] = guard
 
     lane = lax.broadcasted_iota(jnp.int32, (Y, X), 1)
@@ -159,7 +155,7 @@
         if dx:
             if dy == 0:
                 return out.at[pl.ds(at_x, Y)]
-            return out.at[pl.ds(at_lo if dy < 0 else at_x, Z + Y)]
+            return out.at[pl.ds(at_x if dy < 0 else at_x + Y - 8, 8)]
         if dy and dz:
             return out.at[pl.ds((at_lo if dy < 0 else at_hi) + (0 if dz < 0 else Z - 8), 8)]
         if dy:
@@ -247,8 +243,8 @@
         z2 = [zhalo[slot, 0, 0:Y, :], zhalo[slot, 1, Y:2 * Y, :]]
         y2 = [yhalo[slot, 0, Z:2 * Z, :], yhalo[slot, 1, 0:Z, :]]
         zx = [jnp.where(left_half, zxhalo[slot, s, 0], zxhalo[slot, s, 1]) for s in (0, 1)]
-        yx = [jnp.where(left_half, yxhalo[slot, s, 0, r:r + Y, :], yxhalo[slot, s, 1, r:r + Y, :])
-              for s, r in ((0, 0), (1, Z))]
+        yx = [jnp.where(left_half[0:1], yxhalo[slot, s, 0, r:r + 1, :], yxhalo[slot, s, 1, r:r + 1, :])
+              for s, r in ((0, 7), (1, 0))]
         zy = [[zyhalo[slot, sz, sy, r:r + 1, :] for sy in (0, 1)] for sz, r in ((0, 7), (1, 0))]
         uz, uy = [], []
         for s, k in ((0, 0), (1, Z - 1)):
@@ -258,22 +254,21 @@
             total = total + jnp.where(first_y, zy[s][0], pltpu.roll(f, 1, 0))
             total = total + jnp.where(last_y, zy[s][1], pltpu.roll(f, Y - 1, 0))
             uz.append((cz_ref[s] * f - total) * exists["gz"][s])
-        for s, at, r in ((0, at_lo, Y), (1, at_hi, 0)):
+        for s, at in ((0, at_lo), (1, at_hi)):
             f = y1[s]
             total = y2[s] + send[slot, at:at + Z, :]
-            total = total + jnp.where(lane_z == 0, pltpu.roll(yxhalo[slot, s, 0, r:r + Z, :], 1, 1),
-                                      pltpu.roll(f, 1, 1))
-            total = total + jnp.where(lane_z == X - 1,
-                                      pltpu.roll(yxhalo[slot, s, 1, r:r + Z, :], X - 1, 1),
-                                      pltpu.roll(f, X - 1, 1))
+            low, high = (jnp.sum(jnp.where(lane_z == 4 * row_z + j, yx[s], 0.0), axis=1, keepdims=True)
+                         for j in (1, 2))
+            total = total + jnp.where(lane_z == 0, low, pltpu.roll(f, 1, 1))
+            total = total + jnp.where(lane_z == X - 1, high, pltpu.roll(f, X - 1, 1))
             total = total + jnp.where(row_z == 0, zy[0][s], pltpu.roll(f, 1, 0))
             total = total + jnp.where(row_z == Z - 1, zy[1][s], pltpu.roll(f, Z - 1, 0))
             uy.append((cy_ref[s] * f - total) * exists["gy"][s])
         own = send[slot, at_x:at_x + Y, :]
         total = jnp.where(place == 1, pltpu.roll(x1, 1, 1) + pltpu.roll(own, X - 1, 1),
                           pltpu.roll(x1, X - 1, 1) + pltpu.roll(own, 1, 1))
-        total = total + jnp.where(first_y, yx[0][Y - 1:Y, :], pltpu.roll(x1, 1, 0))
-        total = total + jnp.where(last_y, yx[1][0:1, :], pltpu.roll(x1, Y - 1, 0))
+        total = total + jnp.where(first_y, yx[0], pltpu.roll(x1, 1, 0))
+        total = total + jnp.where(last_y, yx[1], pltpu.roll(x1, Y - 1, 0))
         total = total + jnp.where(lane < 4, pltpu.roll(zx[0], 4, 1), pltpu.roll(x1, 4, 1))
         total = total + jnp.where(lane >= X - 4, pltpu.roll(zx[1], X - 4, 1),
                                   pltpu.roll(x1, X - 4, 1))
@@ -326,7 +321,9 @@
     pl.semaphore_wait(barrier, count)
     start_all(2, c_ref, 0)
     loads[1].wait()
-    start_all(0, v_ref.at[0], Y)
+    start_all(0, v, Y)
+    for k in range(Z):
+        v_hist[0, k * Y:(k + 1) * Y, :] = v[Y + k * Y:2 * Y + k * Y, :]
     loads[2].wait()
     finish(False, 2, c_ref, 0)
     finish(True, 2, c_ref, 0)
@@ -373,15 +370,14 @@
     def q_body(q, carry):
         phase = lax.rem(q, half)
         sweep = jnp.minimum(phase, 1)
-        source = sweep * (1 + half * (q // half)) + (1 - sweep) * zero_slot * ((q + last_q - 1) // last_q)
-        sign = jnp.where((sweep == 0) & (q > 0), -1.0, 1.0).astype(jnp.float32)
-        old, new, keep = jnp.float32(0.0), sign * jnp.float32(inv_centre), jnp.float32(0.0)
+        sweeping = (sweep > 0).astype(jnp.float32)
+        sign = jnp.where(q > 0, -1.0, 1.0).astype(jnp.float32)
+        use_src = jnp.where((sweep > 0) | (q == 0), 1.0, 0.0).astype(jnp.float32)
+        take = (1.0 - sweeping) * sign
+        old, new = jnp.float32(0.0), sign * jnp.float32(inv_centre)
         for j, (wo, wn) in enumerate(weights):
             old = jnp.where(phase == j + 1, jnp.float32(wo), old)
             new = jnp.where(phase == j + 1, jnp.float32(wn), new)
-            keep = jnp.where(phase == j + 1, jnp.float32(1.0), keep)
-        v = v_ref.at[q]
-        v_new = v_ref.at[q + 1]
         zero8 = jnp.zeros((8, X), jnp.float32)
         acc = {"u": zero8, "s": zero8, "v": zero8, "x": jnp.zeros((Y, X), jnp.float32)}
 
@@ -397,14 +393,17 @@
             rows = slice(k * Y, (k + 1) * Y)
             vrows = slice(Y + k * Y, 2 * Y + k * Y)
             t = t * inv36
-            src = e_ref[source, rows, :]
-            defect = src - t
-            e_ref[q + 1, rows, :] = sign * defect
+            src = src_ref[rows, :]
+            defect = use_src * src - t
+            kept = sweeping * src + take * defect
+            src_ref[rows, :] = kept
+            s_hist[q, rows, :] = kept
             upd = old * d_ref[rows, :] + new * defect
             d_ref[rows, :] = upd
             was = v[vrows, :]
-            z = keep * was + upd
-            v_new[vrows, :] = z
+            z = sweeping * was + upd
+            v[vrows, :] = z
+            v_hist[q + 1, rows, :] = z
             fold("s", src * z)
             fold("v", was * t)
             acc["x"] = jnp.where(quarter == k, pltpu.roll(z, (2 + 4 * k) % X, 1), acc["x"])
@@ -418,7 +417,7 @@
         finish(True, slot, v, Y)
         k_second(outer(slot, v, Y), post_t)
         send[1 - slot, at_x:at_x + Y, :] = acc["x"]
-        pl.when(q < last_q)(lambda: start_all(1 - slot, v_new, Y, packed_x=True))
+        pl.when(q < last_q)(lambda: start_all(1 - slot, v, Y, packed_x=True))
         sums_s[q] = acc["s"]
         sums_v[q] = acc["v"]
         return carry
@@ -441,25 +440,8 @@
     q = alpha1 * alpha
     for k in range(Z):
         rows = slice(k * Y, (k + 1) * Y)
-        vrows = slice(Y + k * Y, 2 * Y + k * Y)
-        x_ref[rows, :] = v_ref[0, vrows, :] + p * v_ref[half, vrows, :] - q * v_ref[last_q, vrows, :]
-        r_ref[rows, :] = e_ref[1, rows, :] - p * e_ref[half + 1, rows, :] + q * e_ref[last_q + 1, rows, :]
-
-
-PIECES = 4
-
-
-def hand_on(x_in, r_in, x_out, r_out, sem):
-    copies = []
-    for i, (src, dst) in enumerate(((x_in, x_out), (r_in, r_out))):
-        n = src.shape[0] // PIECES
-        for j in range(PIECES):
-            rows = pl.ds(j * n, n)
-            copies.append(pltpu.make_async_copy(src.at[rows], dst.at[rows], sem.at[i, j]))
-    for copy in copies:
-        copy.start()
-    for copy in copies:
-        copy.wait()
+        x_ref[rows, :] = v_hist[0, rows, :] + p * v_hist[half, rows, :] - q * v_hist[last_q, rows, :]
+        r_ref[rows, :] = s_hist[0, rows, :] - p * s_hist[half, rows, :] + q * s_hist[last_q, rows, :]
 
 
 def body(sizes, right_side, initial, kappa_sq):
@@ -480,8 +462,10 @@
         in_specs=[hbm] * 3,
         out_specs=[vm] * 2,
         scratch_shapes=[
-            pltpu.VMEM((count + 1, N + 2 * Y, X), f32),
-            pltpu.VMEM((count + 2, N, X), f32),
+            pltpu.VMEM((N + 2 * Y, X), f32),
+            pltpu.VMEM((N, X), f32),
+            pltpu.VMEM((count + 1, N, X), f32),
+            pltpu.VMEM((count, N, X), f32),
             pltpu.VMEM((N + 2 * Y, X), f32),
             pltpu.VMEM((2, Z, X), f32),
             pltpu.VMEM((N, X), f32),
@@ -492,7 +476,7 @@
             pltpu.VMEM((slots, 2, 2 * Y, X), f32),
             pltpu.VMEM((slots, 2, 2, 8, X), f32),
             pltpu.VMEM((slots, 2, 2, Y, X), f32),
-            pltpu.VMEM((slots, 2, 2, Z + Y, X), f32),
+            pltpu.VMEM((slots, 2, 2, 8, X), f32),
             pltpu.VMEM((2, Y, X), f32),
             pltpu.VMEM((2, Z, X), f32),
             pltpu.VMEM((Y, X), f32),
@@ -511,15 +495,6 @@
             collective_id=0, has_side_effects=True, vmem_limit_bytes=63 * 1024 * 1024),
         name="cg",
     )(flat(right_side), flat(initial), flat(kappa_sq))
-    out = pl.pallas_call(
-        hand_on,
-        out_shape=[jax.ShapeDtypeStruct((N, X), f32)] * 2,
-        in_specs=[hbm] * 2,
-        out_specs=[hbm] * 2,
-        scratch_shapes=[pltpu.SemaphoreType.DMA((2, PIECES))],
-        compiler_params=pltpu.CompilerParams(vmem_limit_bytes=63 * 1024 * 1024),
-        name="hand_on",
-    )(*out)
     return tuple(o.reshape(Z, Y, X) for o in out)
 
 

time: 59.7 us -> 50.2 us (0.84)
  Pallas kernels: 58.9 us -> 47 us
  local copies, waits for them, and re-layouts: 0 us -> 2.42 us
    pallas_call x1 -> x0, Pallas kernels: 17.1 us -> none  [body(): pl.pallas_call(hand_on, out_shape=[jax.ShapeDtypeStruct((N, X), f32)] * 2...]
    pallas_call x1, Pallas kernels: 41.8 us -> 47 us  [body(): pl.pallas_call(functools.partial(kernel, sizes, phases, (Z, Y, X)), out_s...]
    unnamed x0 -> x4, local copies, waits for them, and re-layouts: none -> 2.42 us
where the time goes in v5:
time: 50.2 us; the launch traced here: 50.1 us
  Pallas kernels  47 us (94%)
  local copies, waits for them, and re-layouts  2.42 us (5%)
  between operations  0.65 us (1%)
    pallas_call x1, Pallas kernels, body(): pl.pallas_call(functools.partial(kernel, sizes, phases, (Z, Y, X)), out_s...  47 us
    unnamed x4, local copies, waits for them, and re-layouts  2.42 us

profile of v5, /device:TPU:0, one launch (start us, length us, event | category | flops | bytes accessed | tf_op | source)
XLA Modules:
  0.0 50.1 jit_solution(9372732342331946524)
XLA Ops:
  0.6 47.0 %cg.1 = (f32[512,128]{1,0:T(8,128)}, f32[512,128]{1,0:T(8,128)}) custom-call(f32[512,128]{1,0:T(8,128)} %bitcast.5, f32[512,128]{1,0:T(8,128)} %bitcast.6, f32[512,128]{1,0:T(8,128)} %bitcast.7), custom_call_target="tpu_custom_call" | custom-call | tf_op jit(solution)/shard_map/cg/pallas_call | solution.py:459
  47.6 0.0 copy-start
  47.6 1.7 %copy.7 = f32[32,16,128]{2,1,0:T(8,128)} copy(f32[32,16,128]{2,1,0:T(8,128)} %bitcast.9) | data formatting | bytes 524288
  49.4 0.0 copy-done
  49.4 0.7 %copy.8 = f32[32,16,128]{2,1,0:T(8,128)} copy(f32[32,16,128]{2,1,0:T(8,128)S(1)} %bitcast.8) | data formatting | bytes 524288
Async XLA Ops:
  47.6 1.7 %copy-start = (f32[512,128]{1,0:T(8,128)S(1)}, f32[512,128]{1,0:T(8,128)}, u32[]{:S(2)}) copy-start(f32[512,128]{1,0:T(8,128)} %get-tuple-element.5) | copy-start | bytes 786436

commit v6 on v4

--- a/solution.py
+++ b/solution.py
@@ -55,9 +55,9 @@
 
 
 def kernel(sizes, phases, shape, b_hbm, x0_hbm, kap_hbm, x_ref, r_ref,
-           v_ref, e_ref, u_ref, hrow, c_ref, d_ref,
-           send, xhalo, yhalo, zhalo, zyhalo, zxhalo, yxhalo, cz_ref, cy_ref, cx_ref,
-           sums_s, sums_v, sums_u, part, gather_a, gather_b, gather_c,
+           v_ref, e_ref, u_ref, t_ref, c_ref, d_ref,
+           send, xhalo, yhalo, zhalo, zyhalo, zxhalo, yxhalo, cz_ref, cy_ref, cx_ref, cown_ref,
+           sums_s, sums_v, part, gather_a, gather_b, gather_c,
            send_sem, recv_sem, red_send, red_recv, in_sem):
     Z, Y, X = shape
     N = Z * Y
@@ -289,38 +289,33 @@
             total = total + jnp.where(last_y, 0.0, src[i + 1:i + 1 + Y, :])
             dst[dst_off + k * Y:dst_off + (k + 1) * Y, :] = c_ref[k * Y:(k + 1) * Y, :] * v - total
 
-    def k_first(halo, post):
-        hz, hy, hx = halo
-        for s in (0, 1):
-            hrow[s] = hy[s]
-        pairs = pairs_of(hx)
-        for k in range(Z):
-            total = edge_of(pairs, k)
-            total = total + jnp.where(first_y, hrow[0, k:k + 1, :], 0.0)
-            total = total + jnp.where(last_y, hrow[1, k:k + 1, :], 0.0)
-            if k == 0:
-                total = total + hz[0]
-            if k == Z - 1:
-                total = total + hz[1]
-            post(k, u_ref[Y + k * Y:2 * Y + k * Y, :] - total)
-
-    def k_second(halo, post):
-        hz, hy, hx = halo
-        u_ref[0:Y, :] = hz[0]
-        u_ref[Y + N:2 * Y + N, :] = hz[1]
-        for s in (0, 1):
-            hrow[s] = hy[s]
-        pairs = pairs_of(hx)
-        for k in range(Z):
-            i = Y + k * Y
-            f = u_ref[i:i + Y, :]
-            ends = pltpu.roll(pairs, (2 * X - 2 - 4 * k) % X, 1)
-            total = u_ref[i - Y:i, :] + u_ref[i + Y:i + 2 * Y, :]
-            total = total + jnp.where(first_x, ends, pltpu.roll(f, 1, 1))
-            total = total + jnp.where(last_x, ends, pltpu.roll(f, X - 1, 1))
-            total = total + jnp.where(first_y, hrow[0, k:k + 1, :], u_ref[i - 1:i - 1 + Y, :])
-            total = total + jnp.where(last_y, hrow[1, k:k + 1, :], u_ref[i + 1:i + 1 + Y, :])
-            post(k, c_ref[k * Y:(k + 1) * Y, :] * f - total)
+    def k_edges(halo, beyond):
+        for s, k, inward in ((0, 0, 1), (1, Z - 1, Z - 2)):
+            f = halo[0][s]
+            rows = slice(k * Y, (k + 1) * Y)
+            t_ref[rows, :] = (t_ref[rows, :] - beyond[0][s] - c_ref[rows, :] * f + along_x(f, lane)
+                              + jnp.where(first_y, 0.0, pltpu.roll(f, 1, 0))
+                              + jnp.where(last_y, 0.0, pltpu.roll(f, Y - 1, 0)))
+            rows = slice(inward * Y, (inward + 1) * Y)
+            t_ref[rows, :] = t_ref[rows, :] + f
+        for s, y, inward in ((0, 0, 1), (1, Y - 1, Y - 2)):
+            f = halo[1][s]
+            rows = pl.ds(y, Z, stride=Y)
+            t_ref[rows, :] = (t_ref[rows, :] - beyond[1][s] - c_ref[rows, :] * f + along_x(f, lane_z)
+                              + jnp.where(row_z == 0, 0.0, pltpu.roll(f, 1, 0))
+                              + jnp.where(row_z == Z - 1, 0.0, pltpu.roll(f, Z - 1, 0)))
+            rows = pl.ds(inward, Z, stride=Y)
+            t_ref[rows, :] = t_ref[rows, :] + f
+        f = pairs_of(halo[2])
+        edge = (-pairs_of(beyond[2]) - cown_ref[...] * f
+                + jnp.where(first_y, 0.0, pltpu.roll(f, 1, 0))
+                + jnp.where(last_y, 0.0, pltpu.roll(f, Y - 1, 0))
+                + jnp.where(lane < 4, 0.0, pltpu.roll(f, 4, 1))
+                + jnp.where(lane >= X - 4, 0.0, pltpu.roll(f, X - 4, 1)))
+        return jnp.where(place == 3, pltpu.roll(f, 1, 1),
+                         jnp.where(place == 0, pltpu.roll(f, X - 1, 1), edge))
+
+    two_x = (lane < 2) | (lane >= X - 2)
 
     loads[0].wait()
     pl.semaphore_wait(barrier, count)
@@ -335,6 +330,7 @@
         cz_ref[s] = 6.0 + kz[s]
         cy_ref[s] = 6.0 + ky[s]
     cx_ref[...] = 6.0 + kx
+    cown_ref[...] = 6.0 + send[2, at_x:at_x + Y, :]
     for k in range(Z):
         rows = slice(k * Y, (k + 1) * Y)
         c_ref[rows, :] = 6.0 + c_ref[rows, :]
@@ -366,7 +362,7 @@
     def red_first():
         rows8 = lax.broadcasted_iota(jnp.int32, (8, X), 0)
         mine = jnp.zeros((8, X), jnp.float32)
-        for j, value in enumerate((sums_s[half - 1], sums_v[half], sums_s[last_q - 1], sums_u[...])):
+        for j, value in enumerate((sums_s[half - 1], sums_v[half], sums_s[last_q - 1], sums_v[last_q])):
             mine = jnp.where(rows8 == j, jnp.sum(value, axis=0, keepdims=True), mine)
         red_start(0, mine)
 
@@ -383,15 +379,11 @@
         v = v_ref.at[q]
         v_new = v_ref.at[q + 1]
         zero8 = jnp.zeros((8, X), jnp.float32)
-        acc = {"u": zero8, "s": zero8, "v": zero8, "x": jnp.zeros((Y, X), jnp.float32)}
+        acc = {"s": zero8, "v": zero8, "x": jnp.zeros((Y, X), jnp.float32)}
 
         def fold(name, value):
             for j in range(0, Y, 8):
                 acc[name] = acc[name] + value[j:j + 8]
-
-        def post_u(k, value):
-            u_ref[Y + k * Y:2 * Y + k * Y, :] = value
-            fold("u", value * value)
 
         def post_t(k, t):
             rows = slice(k * Y, (k + 1) * Y)
@@ -411,12 +403,13 @@
 
         slot = lax.rem(q, 2)
         k_inner(v, u_ref, Y)
+        k_inner(u_ref, t_ref, 0)
         finish(False, slot, v, Y)
-        k_first(faces(slot), post_u)
-        sums_u[...] = acc["u"]
-        pl.when(q == last_q)(red_first)
         finish(True, slot, v, Y)
-        k_second(outer(slot, v, Y), post_t)
+        columns = k_edges(faces(slot), outer(slot, v, Y))
+        for k in range(Z):
+            fix = jnp.where(two_x, pltpu.roll(columns, (2 * X - 2 - 4 * k) % X, 1), 0.0)
+            post_t(k, t_ref[k * Y:(k + 1) * Y, :] + fix)
         send[1 - slot, at_x:at_x + Y, :] = acc["x"]
         pl.when(q < last_q)(lambda: start_all(1 - slot, v_new, Y, packed_x=True))
         sums_s[q] = acc["s"]
@@ -425,13 +418,14 @@
 
     lax.fori_loop(0, last_q + 1, q_body, 0)
 
+    red_first()
     total = red_finish(0)
     for i in range(1, len(phases)):
         red_start(i, total)
         total = red_finish(i)
     totals = jnp.sum(total, axis=1, keepdims=True)
     e0, g1, g2 = totals[0:1], totals[1:2], totals[2:3]
-    g3 = totals[3:4] * inv36
+    g3 = totals[3:4]
     alpha = e0 / g1
     e1 = e0 - 2.0 * alpha * g1 + alpha * alpha * g2
     keep = 1.0 + e1 / e0
@@ -444,22 +438,6 @@
         vrows = slice(Y + k * Y, 2 * Y + k * Y)
         x_ref[rows, :] = v_ref[0, vrows, :] + p * v_ref[half, vrows, :] - q * v_ref[last_q, vrows, :]
         r_ref[rows, :] = e_ref[1, rows, :] - p * e_ref[half + 1, rows, :] + q * e_ref[last_q + 1, rows, :]
-
-
-PIECES = 4
-
-
-def hand_on(x_in, r_in, x_out, r_out, sem):
-    copies = []
-    for i, (src, dst) in enumerate(((x_in, x_out), (r_in, r_out))):
-        n = src.shape[0] // PIECES
-        for j in range(PIECES):
-            rows = pl.ds(j * n, n)
-            copies.append(pltpu.make_async_copy(src.at[rows], dst.at[rows], sem.at[i, j]))
-    for copy in copies:
-        copy.start()
-    for copy in copies:
-        copy.wait()
 
 
 def body(sizes, right_side, initial, kappa_sq):
@@ -483,7 +461,7 @@
             pltpu.VMEM((count + 1, N + 2 * Y, X), f32),
             pltpu.VMEM((count + 2, N, X), f32),
             pltpu.VMEM((N + 2 * Y, X), f32),
-            pltpu.VMEM((2, Z, X), f32),
+            pltpu.VMEM((N, X), f32),
             pltpu.VMEM((N, X), f32),
             pltpu.VMEM((N, X), f32),
             pltpu.VMEM((slots, 4 * Z + Y, X), f32),
@@ -496,9 +474,9 @@
             pltpu.VMEM((2, Y, X), f32),
             pltpu.VMEM((2, Z, X), f32),
             pltpu.VMEM((Y, X), f32),
+            pltpu.VMEM((Y, X), f32),
             pltpu.VMEM((count, 8, X), f32),
             pltpu.VMEM((count, 8, X), f32),
-            pltpu.VMEM((8, X), f32),
             pltpu.VMEM((3, 8, X), f32),
         ] + [pltpu.VMEM(((groups + [1])[i], 8, X), f32) for i in range(3)] + [
             pltpu.SemaphoreType.DMA((slots, len(DIRECTIONS))),
@@ -511,15 +489,6 @@
             collective_id=0, has_side_effects=True, vmem_limit_bytes=63 * 1024 * 1024),
         name="cg",
     )(flat(right_side), flat(initial), flat(kappa_sq))
-    out = pl.pallas_call(
-        hand_on,
-        out_shape=[jax.ShapeDtypeStruct((N, X), f32)] * 2,
-        in_specs=[hbm] * 2,
-        out_specs=[hbm] * 2,
-        scratch_shapes=[pltpu.SemaphoreType.DMA((2, PIECES))],
-        compiler_params=pltpu.CompilerParams(vmem_limit_bytes=63 * 1024 * 1024),
-        name="hand_on",
-    )(*out)
     return tuple(o.reshape(Z, Y, X) for o in out)
 
 

time: 59.7 us -> 45 us (0.75)
  Pallas kernels: 58.9 us -> 41.7 us
  local copies, waits for them, and re-layouts: 0 us -> 2.42 us
    pallas_call x1 -> x0, Pallas kernels: 17.1 us -> none  [body(): pl.pallas_call(hand_on, out_shape=[jax.ShapeDtypeStruct((N, X), f32)] * 2...]
    unnamed x0 -> x4, local copies, waits for them, and re-layouts: none -> 2.42 us
where the time goes in v6:
time: 45 us; the launch traced here: 44.8 us
  Pallas kernels  41.7 us (93%)
  local copies, waits for them, and re-layouts  2.42 us (5%)
  between operations  0.65 us (1%)
    pallas_call x1, Pallas kernels, body(): pl.pallas_call(functools.partial(kernel, sizes, phases, (Z, Y, X)), out_s...  41.7 us
    unnamed x4, local copies, waits for them, and re-layouts  2.42 us

profile of v6, /device:TPU:0, one launch (start us, length us, event | category | flops | bytes accessed | tf_op | source)
XLA Modules:
  0.0 44.8 jit_solution(3501259686191142350)
XLA Ops:
  0.6 41.7 %cg.1 = (f32[512,128]{1,0:T(8,128)}, f32[512,128]{1,0:T(8,128)}) custom-call(f32[512,128]{1,0:T(8,128)} %bitcast.5, f32[512,128]{1,0:T(8,128)} %bitcast.6, f32[512,128]{1,0:T(8,128)} %bitcast.7), custom_call_target="tpu_custom_call" | custom-call | tf_op jit(solution)/shard_map/cg/pallas_call | solution.py:455
  42.4 0.0 copy-start
  42.4 1.7 %copy.7 = f32[32,16,128]{2,1,0:T(8,128)} copy(f32[32,16,128]{2,1,0:T(8,128)} %bitcast.9) | data formatting | bytes 524288
  44.1 0.0 copy-done
  44.1 0.7 %copy.8 = f32[32,16,128]{2,1,0:T(8,128)} copy(f32[32,16,128]{2,1,0:T(8,128)S(1)} %bitcast.8) | data formatting | bytes 524288
Async XLA Ops:
  42.4 1.7 %copy-start = (f32[512,128]{1,0:T(8,128)S(1)}, f32[512,128]{1,0:T(8,128)}, u32[]{:S(2)}) copy-start(f32[512,128]{1,0:T(8,128)} %get-tuple-element.5) | copy-start | bytes 786436

commit v7 on v6

--- a/solution.py
+++ b/solution.py
@@ -56,7 +56,7 @@
 
 def kernel(sizes, phases, shape, b_hbm, x0_hbm, kap_hbm, x_ref, r_ref,
            v_ref, e_ref, u_ref, t_ref, c_ref, d_ref,
-           send, xhalo, yhalo, zhalo, zyhalo, zxhalo, yxhalo, cz_ref, cy_ref, cx_ref, cown_ref,
+           send, xhalo, yhalo, zhalo, zyhalo, zxhalo, yxhalo, cz_ref, cy_ref, cx_ref,
            sums_s, sums_v, part, gather_a, gather_b, gather_c,
            send_sem, recv_sem, red_send, red_recv, in_sem):
     Z, Y, X = shape
@@ -159,7 +159,7 @@
         if dx:
             if dy == 0:
                 return out.at[pl.ds(at_x, Y)]
-            return out.at[pl.ds(at_lo if dy < 0 else at_x, Z + Y)]
+            return out.at[pl.ds(at_x if dy < 0 else at_x + Y - 8, 8)]
         if dy and dz:
             return out.at[pl.ds((at_lo if dy < 0 else at_hi) + (0 if dz < 0 else Z - 8), 8)]
         if dy:
@@ -195,10 +195,10 @@
             send_sem=send_sem.at[slot, i], recv_sem=recv_sem.at[slot, i],
             device_id=offset(d), device_id_type=MESH)
 
-    def start_all(slot, src, off, packed_x=False):
+    def start_all(slot, src, off, packed_x=False, edges=True):
         def go(want):
             for d in DIRS:
-                if want(d):
+                if want(d) and (edges or sum(1 for s in d if s) == 1):
                     when(has(d), lambda d=d: copy_to(d, slot, src, off).start())
 
         if packed_x:
@@ -230,10 +230,8 @@
         return z1, y1, x1
 
     def pairs_of(columns):
-        return jnp.where(place == 2, pltpu.roll(columns, 1, 1), pltpu.roll(columns, X - 1, 1))
-
-    def edge_of(pairs, k):
-        return jnp.where(edge_x, pltpu.roll(pairs, (2 * X - 2 - 4 * k) % X, 1), 0.0)
+        return jnp.where(place[0:columns.shape[0]] == 2,
+                         pltpu.roll(columns, 1, 1), pltpu.roll(columns, X - 1, 1))
 
     def along_x(v, lanes):
         return (jnp.where(lanes == 0, 0.0, pltpu.roll(v, 1, 1))
@@ -242,43 +240,9 @@
     exists = {a: [jnp.where(me[a] > 0, 1.0, 0.0).astype(jnp.float32),
                   jnp.where(me[a] < sizes[a] - 1, 1.0, 0.0).astype(jnp.float32)] for a in AXES}
 
-    def outer(slot, v, off):
-        z1, y1, x1 = faces(slot)
-        z2 = [zhalo[slot, 0, 0:Y, :], zhalo[slot, 1, Y:2 * Y, :]]
-        y2 = [yhalo[slot, 0, Z:2 * Z, :], yhalo[slot, 1, 0:Z, :]]
-        zx = [jnp.where(left_half, zxhalo[slot, s, 0], zxhalo[slot, s, 1]) for s in (0, 1)]
-        yx = [jnp.where(left_half, yxhalo[slot, s, 0, r:r + Y, :], yxhalo[slot, s, 1, r:r + Y, :])
-              for s, r in ((0, 0), (1, Z))]
-        zy = [[zyhalo[slot, sz, sy, r:r + 1, :] for sy in (0, 1)] for sz, r in ((0, 7), (1, 0))]
-        uz, uy = [], []
-        for s, k in ((0, 0), (1, Z - 1)):
-            f = z1[s]
-            total = z2[s] + v[off + k * Y:off + (k + 1) * Y, :] + along_x(f, lane)
-            total = total + edge_of(pairs_of(zx[s]), Z - 1 - k)
-            total = total + jnp.where(first_y, zy[s][0], pltpu.roll(f, 1, 0))
-            total = total + jnp.where(last_y, zy[s][1], pltpu.roll(f, Y - 1, 0))
-            uz.append((cz_ref[s] * f - total) * exists["gz"][s])
-        for s, at, r in ((0, at_lo, Y), (1, at_hi, 0)):
-            f = y1[s]
-            total = y2[s] + send[slot, at:at + Z, :]
-            total = total + jnp.where(lane_z == 0, pltpu.roll(yxhalo[slot, s, 0, r:r + Z, :], 1, 1),
-                                      pltpu.roll(f, 1, 1))
-            total = total + jnp.where(lane_z == X - 1,
-                                      pltpu.roll(yxhalo[slot, s, 1, r:r + Z, :], X - 1, 1),
-                                      pltpu.roll(f, X - 1, 1))
-            total = total + jnp.where(row_z == 0, zy[0][s], pltpu.roll(f, 1, 0))
-            total = total + jnp.where(row_z == Z - 1, zy[1][s], pltpu.roll(f, Z - 1, 0))
-            uy.append((cy_ref[s] * f - total) * exists["gy"][s])
-        own = send[slot, at_x:at_x + Y, :]
-        total = jnp.where(place == 1, pltpu.roll(x1, 1, 1) + pltpu.roll(own, X - 1, 1),
-                          pltpu.roll(x1, X - 1, 1) + pltpu.roll(own, 1, 1))
-        total = total + jnp.where(first_y, yx[0][Y - 1:Y, :], pltpu.roll(x1, 1, 0))
-        total = total + jnp.where(last_y, yx[1][0:1, :], pltpu.roll(x1, Y - 1, 0))
-        total = total + jnp.where(lane < 4, pltpu.roll(zx[0], 4, 1), pltpu.roll(x1, 4, 1))
-        total = total + jnp.where(lane >= X - 4, pltpu.roll(zx[1], X - 4, 1),
-                                  pltpu.roll(x1, X - 4, 1))
-        ux = (cx_ref[...] * x1 - total) * jnp.where(left_half, exists["gx"][0], exists["gx"][1])
-        return uz, uy, ux
+    def along_y(f):
+        return (jnp.where(first_y, 0.0, pltpu.roll(f, 1, 0))
+                + jnp.where(last_y, 0.0, pltpu.roll(f, Y - 1, 0)))
 
     def k_inner(src, dst, dst_off):
         for k in range(Z):
@@ -289,29 +253,40 @@
             total = total + jnp.where(last_y, 0.0, src[i + 1:i + 1 + Y, :])
             dst[dst_off + k * Y:dst_off + (k + 1) * Y, :] = c_ref[k * Y:(k + 1) * Y, :] * v - total
 
-    def k_edges(halo, beyond):
+    def k_edges(slot, v, off):
+        z1, y1, x1 = faces(slot)
+        z2 = [zhalo[slot, 0, 0:Y, :], zhalo[slot, 1, Y:2 * Y, :]]
+        y2 = [yhalo[slot, 0, Z:2 * Z, :], yhalo[slot, 1, 0:Z, :]]
+        zx = [pairs_of(jnp.where(left_half, zxhalo[slot, s, 0], zxhalo[slot, s, 1])) for s in (0, 1)]
+        yx = [pairs_of(jnp.where(left_half[0:8], yxhalo[slot, s, 0], yxhalo[slot, s, 1]))
+              for s in (0, 1)]
+        zy = [[zyhalo[slot, sz, sy, r:r + 1, :] for sy in (0, 1)] for sz, r in ((0, 7), (1, 0))]
         for s, k, inward in ((0, 0, 1), (1, Z - 1, Z - 2)):
-            f = halo[0][s]
+            f = z1[s]
             rows = slice(k * Y, (k + 1) * Y)
-            t_ref[rows, :] = (t_ref[rows, :] - beyond[0][s] - c_ref[rows, :] * f + along_x(f, lane)
-                              + jnp.where(first_y, 0.0, pltpu.roll(f, 1, 0))
-                              + jnp.where(last_y, 0.0, pltpu.roll(f, Y - 1, 0)))
+            own = v[off + k * Y:off + (k + 1) * Y, :] * exists["gz"][s]
+            side = along_x(f, lane) + along_y(f)
+            t_ref[rows, :] = t_ref[rows, :] + (z2[s] + own + 2.0 * side - cz_ref[s] * f)
             rows = slice(inward * Y, (inward + 1) * Y)
             t_ref[rows, :] = t_ref[rows, :] + f
-        for s, y, inward in ((0, 0, 1), (1, Y - 1, Y - 2)):
-            f = halo[1][s]
+        for s, y, inward, at in ((0, 0, 1, at_lo), (1, Y - 1, Y - 2, at_hi)):
+            f = y1[s]
             rows = pl.ds(y, Z, stride=Y)
-            t_ref[rows, :] = (t_ref[rows, :] - beyond[1][s] - c_ref[rows, :] * f + along_x(f, lane_z)
-                              + jnp.where(row_z == 0, 0.0, pltpu.roll(f, 1, 0))
-                              + jnp.where(row_z == Z - 1, 0.0, pltpu.roll(f, Z - 1, 0)))
+            own = send[slot, at:at + Z, :] * exists["gy"][s]
+            side = along_x(f, lane_z)
+            side = side + jnp.where(row_z == 0, zy[0][s], pltpu.roll(f, 1, 0))
+            side = side + jnp.where(row_z == Z - 1, zy[1][s], pltpu.roll(f, Z - 1, 0))
+            t_ref[rows, :] = t_ref[rows, :] + (y2[s] + own + 2.0 * side - cy_ref[s] * f)
             rows = pl.ds(inward, Z, stride=Y)
             t_ref[rows, :] = t_ref[rows, :] + f
-        f = pairs_of(halo[2])
-        edge = (-pairs_of(beyond[2]) - cown_ref[...] * f
-                + jnp.where(first_y, 0.0, pltpu.roll(f, 1, 0))
-                + jnp.where(last_y, 0.0, pltpu.roll(f, Y - 1, 0))
-                + jnp.where(lane < 4, 0.0, pltpu.roll(f, 4, 1))
-                + jnp.where(lane >= X - 4, 0.0, pltpu.roll(f, X - 4, 1)))
+        f = pairs_of(x1)
+        x2 = jnp.where(place == 2, pltpu.roll(x1, 2, 1), pltpu.roll(x1, X - 2, 1))
+        own = send[slot, at_x:at_x + Y, :] * jnp.where(place == 2, exists["gx"][0], exists["gx"][1])
+        side = jnp.where(first_y, yx[0][7:8, :], pltpu.roll(f, 1, 0))
+        side = side + jnp.where(last_y, yx[1][0:1, :], pltpu.roll(f, Y - 1, 0))
+        side = side + jnp.where(lane < 4, pltpu.roll(zx[0], 4, 1), pltpu.roll(f, 4, 1))
+        side = side + jnp.where(lane >= X - 4, pltpu.roll(zx[1], X - 4, 1), pltpu.roll(f, X - 4, 1))
+        edge = x2 + own + 2.0 * side - cx_ref[...] * f
         return jnp.where(place == 3, pltpu.roll(f, 1, 1),
                          jnp.where(place == 0, pltpu.roll(f, X - 1, 1), edge))
 
@@ -319,18 +294,16 @@
 
     loads[0].wait()
     pl.semaphore_wait(barrier, count)
-    start_all(2, c_ref, 0)
+    start_all(2, c_ref, 0, edges=False)
     loads[1].wait()
     start_all(0, v_ref.at[0], Y)
     loads[2].wait()
     finish(False, 2, c_ref, 0)
-    finish(True, 2, c_ref, 0)
     kz, ky, kx = faces(2)
-    for s in (0, 1):
-        cz_ref[s] = 6.0 + kz[s]
-        cy_ref[s] = 6.0 + ky[s]
-    cx_ref[...] = 6.0 + kx
-    cown_ref[...] = 6.0 + send[2, at_x:at_x + Y, :]
+    for s, k, at in ((0, 0, at_lo), (1, Z - 1, at_hi)):
+        cz_ref[s] = 12.0 + kz[s] + c_ref[k * Y:(k + 1) * Y, :]
+        cy_ref[s] = 12.0 + ky[s] + send[2, at:at + Z, :]
+    cx_ref[...] = 12.0 + pairs_of(kx) + send[2, at_x:at_x + Y, :]
     for k in range(Z):
         rows = slice(k * Y, (k + 1) * Y)
         c_ref[rows, :] = 6.0 + c_ref[rows, :]
@@ -406,7 +379,7 @@
         k_inner(u_ref, t_ref, 0)
         finish(False, slot, v, Y)
         finish(True, slot, v, Y)
-        columns = k_edges(faces(slot), outer(slot, v, Y))
+        columns = k_edges(slot, v, Y)
         for k in range(Z):
             fix = jnp.where(two_x, pltpu.roll(columns, (2 * X - 2 - 4 * k) % X, 1), 0.0)
             post_t(k, t_ref[k * Y:(k + 1) * Y, :] + fix)
@@ -470,10 +443,9 @@
             pltpu.VMEM((slots, 2, 2 * Y, X), f32),
             pltpu.VMEM((slots, 2, 2, 8, X), f32),
             pltpu.VMEM((slots, 2, 2, Y, X), f32),
-            pltpu.VMEM((slots, 2, 2, Z + Y, X), f32),
+            pltpu.VMEM((slots, 2, 2, 8, X), f32),
             pltpu.VMEM((2, Y, X), f32),
             pltpu.VMEM((2, Z, X), f32),
-            pltpu.VMEM((Y, X), f32),
             pltpu.VMEM((Y, X), f32),
             pltpu.VMEM((count, 8, X), f32),
             pltpu.VMEM((count, 8, X), f32),

time: 45 us -> 44.4 us (0.987)
  Pallas kernels: 41.7 us -> 41.2 us
    pallas_call x1, Pallas kernels: 41.7 us -> 41.2 us  [body(): pl.pallas_call(functools.partial(kernel, sizes, phases, (Z, Y, X)), out_s...]
where the time goes in v7:
time: 44.4 us; the launch traced here: 44.3 us
  Pallas kernels  41.2 us (93%)
  local copies, waits for them, and re-layouts  2.42 us (5%)
  between operations  0.65 us (1%)
    pallas_call x1, Pallas kernels, body(): pl.pallas_call(functools.partial(kernel, sizes, phases, (Z, Y, X)), out_s...  41.2 us
    unnamed x4, local copies, waits for them, and re-layouts  2.42 us

profile of v7, /device:TPU:0, one launch (start us, length us, event | category | flops | bytes accessed | tf_op | source)
XLA Modules:
  0.0 44.3 jit_solution(6224361162724550612)
XLA Ops:
  0.6 41.2 %cg.1 = (f32[512,128]{1,0:T(8,128)}, f32[512,128]{1,0:T(8,128)}) custom-call(f32[512,128]{1,0:T(8,128)} %bitcast.5, f32[512,128]{1,0:T(8,128)} %bitcast.6, f32[512,128]{1,0:T(8,128)} %bitcast.7), custom_call_target="tpu_custom_call" | custom-call | tf_op jit(solution)/shard_map/cg/pallas_call | solution.py:428
  41.9 0.0 copy-start
  41.9 1.7 %copy.7 = f32[32,16,128]{2,1,0:T(8,128)} copy(f32[32,16,128]{2,1,0:T(8,128)} %bitcast.9) | data formatting | bytes 524288
  43.6 0.0 copy-done
  43.6 0.7 %copy.8 = f32[32,16,128]{2,1,0:T(8,128)} copy(f32[32,16,128]{2,1,0:T(8,128)S(1)} %bitcast.8) | data formatting | bytes 524288
Async XLA Ops:
  41.9 1.7 %copy-start = (f32[512,128]{1,0:T(8,128)S(1)}, f32[512,128]{1,0:T(8,128)}, u32[]{:S(2)}) copy-start(f32[512,128]{1,0:T(8,128)} %get-tuple-element.5) | copy-start | bytes 786436

commit v8 on v7

--- a/solution.py
+++ b/solution.py
@@ -7,6 +7,7 @@
 from jax.sharding import PartitionSpec as P
 
 SWEEPS = 3
+GROUP = 4
 cheb_high = 7.2
 cheb_low = 0.072
 MESH = pl.DeviceIdType.MESH
@@ -245,13 +246,17 @@
                 + jnp.where(last_y, 0.0, pltpu.roll(f, Y - 1, 0)))
 
     def k_inner(src, dst, dst_off):
-        for k in range(Z):
-            i = Y + k * Y
-            v = src[i:i + Y, :]
-            total = src[i - Y:i, :] + src[i + Y:i + 2 * Y, :] + along_x(v, lane)
-            total = total + jnp.where(first_y, 0.0, src[i - 1:i - 1 + Y, :])
-            total = total + jnp.where(last_y, 0.0, src[i + 1:i + 1 + Y, :])
-            dst[dst_off + k * Y:dst_off + (k + 1) * Y, :] = c_ref[k * Y:(k + 1) * Y, :] * v - total
+        for base in range(0, Z, GROUP):
+            done = []
+            for k in range(base, min(base + GROUP, Z)):
+                i = Y + k * Y
+                v = src[i:i + Y, :]
+                total = src[i - Y:i, :] + src[i + Y:i + 2 * Y, :] + along_x(v, lane)
+                total = total + jnp.where(first_y, 0.0, src[i - 1:i - 1 + Y, :])
+                total = total + jnp.where(last_y, 0.0, src[i + 1:i + 1 + Y, :])
+                done.append((k, c_ref[k * Y:(k + 1) * Y, :] * v - total))
+            for k, value in done:
+                dst[dst_off + k * Y:dst_off + (k + 1) * Y, :] = value
 
     def k_edges(slot, v, off):
         z1, y1, x1 = faces(slot)
@@ -364,15 +369,18 @@
             t = t * inv36
             src = e_ref[source, rows, :]
             defect = src - t
-            e_ref[q + 1, rows, :] = sign * defect
             upd = old * d_ref[rows, :] + new * defect
-            d_ref[rows, :] = upd
             was = v[vrows, :]
             z = keep * was + upd
-            v_new[vrows, :] = z
             fold("s", src * z)
             fold("v", was * t)
             acc["x"] = jnp.where(quarter == k, pltpu.roll(z, (2 + 4 * k) % X, 1), acc["x"])
+
+            def store():
+                e_ref[q + 1, rows, :] = sign * defect
+                d_ref[rows, :] = upd
+                v_new[vrows, :] = z
+            return store
 
         slot = lax.rem(q, 2)
         k_inner(v, u_ref, Y)
@@ -380,9 +388,13 @@
         finish(False, slot, v, Y)
         finish(True, slot, v, Y)
         columns = k_edges(slot, v, Y)
-        for k in range(Z):
-            fix = jnp.where(two_x, pltpu.roll(columns, (2 * X - 2 - 4 * k) % X, 1), 0.0)
-            post_t(k, t_ref[k * Y:(k + 1) * Y, :] + fix)
+        for base in range(0, Z, GROUP):
+            stores = []
+            for k in range(base, min(base + GROUP, Z)):
+                fix = jnp.where(two_x, pltpu.roll(columns, (2 * X - 2 - 4 * k) % X, 1), 0.0)
+                stores.append(post_t(k, t_ref[k * Y:(k + 1) * Y, :] + fix))
+            for store in stores:
+                store()
         send[1 - slot, at_x:at_x + Y, :] = acc["x"]
         pl.when(q < last_q)(lambda: start_all(1 - slot, v_new, Y, packed_x=True))
         sums_s[q] = acc["s"]

time: 44.4 us -> 43.7 us (0.984)
  Pallas kernels: 41.2 us -> 40.5 us
    pallas_call x1, Pallas kernels: 41.2 us -> 40.5 us  [body(): pl.pallas_call(functools.partial(kernel, sizes, phases, (Z, Y, X)), out_s...]
where the time goes in v8:
time: 43.7 us; the launch traced here: 43.6 us
  Pallas kernels  40.5 us (93%)
  local copies, waits for them, and re-layouts  2.42 us (6%)
  between operations  0.65 us (1%)
    pallas_call x1, Pallas kernels, body(): pl.pallas_call(functools.partial(kernel, sizes, phases, (Z, Y, X)), out_s...  40.5 us
    unnamed x4, local copies, waits for them, and re-layouts  2.42 us

profile of v8, /device:TPU:0, one launch (start us, length us, event | category | flops | bytes accessed | tf_op | source)
XLA Modules:
  0.0 43.6 jit_solution(16237714406460081173)
XLA Ops:
  0.6 40.5 %cg.1 = (f32[512,128]{1,0:T(8,128)}, f32[512,128]{1,0:T(8,128)}) custom-call(f32[512,128]{1,0:T(8,128)} %bitcast.5, f32[512,128]{1,0:T(8,128)} %bitcast.6, f32[512,128]{1,0:T(8,128)} %bitcast.7), custom_call_target="tpu_custom_call" | custom-call | tf_op jit(solution)/shard_map/cg/pallas_call | solution.py:440
  41.1 0.0 copy-start
  41.2 1.7 %copy.7 = f32[32,16,128]{2,1,0:T(8,128)} copy(f32[32,16,128]{2,1,0:T(8,128)} %bitcast.9) | data formatting | bytes 524288
  42.9 0.0 copy-done
  42.9 0.7 %copy.8 = f32[32,16,128]{2,1,0:T(8,128)} copy(f32[32,16,128]{2,1,0:T(8,128)S(1)} %bitcast.8) | data formatting | bytes 524288
Async XLA Ops:
  41.1 1.7 %copy-start = (f32[512,128]{1,0:T(8,128)S(1)}, f32[512,128]{1,0:T(8,128)}, u32[]{:S(2)}) copy-start(f32[512,128]{1,0:T(8,128)} %get-tuple-element.5) | copy-start | bytes 786436
